TPU v7x, 1024 devices: a whole 8x8x8 slice. The times are simulated.
1024 devices in a mesh: seq: 64 (over y, z_hi, core), dp: 16 (over z_lo, x).
Axes of the slice: x: 8, y: 8, z: 8 (z_hi: 4, z_lo: 2; z = z_hi * 2 + z_lo), core: 2. Of those that a mesh axis runs over, the one named last changes fastest.
Arguments:
- projected: bfloat16 [3, 32768, 4096], P(None, 'seq', 'dp'), may hold values from -6 to 6
- featurizer: bfloat16 [7, 3, 4096], P(None, None, 'dp'), may hold values from -25 to 25
- long_filter: bfloat16 [256, 128], P('dp'), may hold values from -0.5 to 0.5
- skip_gain: bfloat16 [4096], P('dp'), may hold values from -4 to 4
- out_cotangent: bfloat16 [32768, 4096], P('seq', 'dp'), may hold values from -6 to 6
Outputs:
- grad_featurizer: float32 [7, 3, 4096], P(None, None, 'dp')
- grad_filter: float32 [256, 128], P('dp')
- grad_skip: float32 [4096], P('dp')
All inputs are finite; a program needn't handle non-finite values.
Results may differ from a plain program's by a relative error of at most 0.0071.
Values may be sent and summed in bfloat16 or wider, within the bound.
A program may use at most 32 MiB of HBM per device.

v0:
```python
import math

import jax
import jax.numpy as jnp
from jax import lax
from jax.sharding import PartitionSpec as P


def shifted(array, axis, by):
    length = lax.axis_size(axis)
    pairs = [(i, i + by) for i in range(length) if 0 <= i + by < length]
    return lax.ppermute(array, axis, pairs)


def band_matrix(taps, block_rows):
    groups, filter_taps = taps.shape
    width = block_rows + filter_taps - 1
    pattern = jnp.concatenate([taps, jnp.zeros((groups, block_rows), taps.dtype)], axis=1)
    tiled = jnp.tile(pattern, (1, block_rows))[:, : block_rows * width]
    shaped = tiled.reshape(groups, block_rows, width)
    return jnp.concatenate([shaped, jnp.zeros((groups, block_rows, 1), taps.dtype)], axis=2)


def window_blocks(source, block_rows, filter_taps, groups):
    rows, channels = source.shape
    blocks_out = (rows - filter_taps + 1) // block_rows
    total_rows = (blocks_out + 1) * block_rows
    padded = jnp.concatenate(
        [source, jnp.zeros((total_rows - rows, channels), source.dtype)], axis=0
    )
    shaped = padded.reshape(blocks_out + 1, block_rows, groups, channels // groups)
    return (shaped[:-1], shaped[1:, :filter_taps])


def apply_band(taps, source, block_rows):
    groups, filter_taps = taps.shape
    channels = source.shape[1]
    left, right = window_blocks(source, block_rows, filter_taps, groups)
    blocks_out = left.shape[0]
    step = math.gcd(groups, 4)

    def apply_one_step(number):
        part_taps = lax.dynamic_slice_in_dim(taps, number * step, step, 0)
        band = band_matrix(part_taps, block_rows)
        part_left = lax.dynamic_slice_in_dim(left, number * step, step, 2)
        part_right = lax.dynamic_slice_in_dim(right, number * step, step, 2)
        near = jnp.einsum(
            "gts,bsgi->btgi", band[:, :, :block_rows], part_left, preferred_element_type=jnp.float32
        )
        far = jnp.einsum(
            "gts,bsgi->btgi",
            band[:, :, block_rows:],
            part_right,
            preferred_element_type=jnp.float32,
        )
        return near + far

    pieces = lax.map(apply_one_step, jnp.arange(groups // step))
    return jnp.moveaxis(pieces, 0, 2).reshape(blocks_out * block_rows, channels)


def filter_gradient(cotangent, source, filter_taps, groups, block_rows):
    rows, channels = cotangent.shape
    members = channels // groups
    left, right = window_blocks(source, block_rows, filter_taps, groups)
    blocks_out = left.shape[0]
    cot_blocks = cotangent.reshape(blocks_out, block_rows, groups, members)
    step = math.gcd(groups, 4)
    span = block_rows + filter_taps

    def filter_one_step(number):
        part_cot = lax.dynamic_slice_in_dim(cot_blocks, number * step, step, 2)
        part_left = lax.dynamic_slice_in_dim(left, number * step, step, 2)
        part_right = lax.dynamic_slice_in_dim(right, number * step, step, 2)
        near = jnp.einsum("btgi,bsgi->gts", part_cot, part_left, preferred_element_type=jnp.float32)
        far = jnp.einsum("btgi,bsgi->gts", part_cot, part_right, preferred_element_type=jnp.float32)
        full = jnp.concatenate([near, far], axis=2)
        flat = full.reshape(step, block_rows * span)
        flat = jnp.concatenate([flat, jnp.zeros((step, block_rows), jnp.float32)], axis=1)
        diagonal = flat.reshape(step, block_rows, span + 1)[:, :, :filter_taps]
        return jnp.sum(diagonal, axis=1)

    stacked = lax.map(filter_one_step, jnp.arange(groups // step)).reshape(groups, filter_taps)
    return jnp.flip(stacked, 1)


def body(projected, featurizer, long_filter, skip_gain, out_cotangent):
    parts, local_rows, channels = projected.shape
    groups, filter_taps = long_filter.shape
    feat_taps = featurizer.shape[0]
    block_rows = min(local_rows, 256)
    feat_f32 = featurizer.astype(jnp.float32)
    reach = feat_taps - 1 + filter_taps - 1
    raw_rim = shifted(projected[:, local_rows - reach :, :], "seq", 1)
    input_rim = raw_rim[:, filter_taps - 1 :, :]
    rim_f32 = feat_f32[0, 1:, None, :] * raw_rim[1:, feat_taps - 1 :, :].astype(jnp.float32)
    for tap_index in range(1, feat_taps):
        begin = feat_taps - 1 - tap_index
        rim_f32 = rim_f32 + feat_f32[tap_index, 1:, None, :] * raw_rim[
            1:, begin : begin + filter_taps - 1, :
        ].astype(jnp.float32)
    rim_featured = rim_f32.astype(jnp.bfloat16)
    product_rim = (
        rim_featured[0].astype(jnp.float32) * rim_featured[1].astype(jnp.float32)
    ).astype(jnp.bfloat16)
    extended = jnp.concatenate([input_rim, projected], axis=1)
    featured_f32 = feat_f32[0][:, None, :] * projected.astype(jnp.float32)
    for tap_index in range(1, feat_taps):
        begin = feat_taps - 1 - tap_index
        featured_f32 = featured_f32 + feat_f32[tap_index][:, None, :] * extended[
            :, begin : begin + local_rows, :
        ].astype(jnp.float32)
    featured = featured_f32.astype(jnp.bfloat16)
    queries_f32 = featured[0].astype(jnp.float32)
    key_f32 = featured[1].astype(jnp.float32)
    value_f32 = featured[2].astype(jnp.float32)
    product = (key_f32 * value_f32).astype(jnp.bfloat16)
    forward_source = jnp.concatenate([product_rim, product], axis=0)
    filtered = apply_band(jnp.flip(long_filter, 1), forward_source, block_rows)
    skip_f32 = skip_gain.astype(jnp.float32)
    product_f32 = product.astype(jnp.float32)
    inner_sum = filtered + skip_f32 * product_f32
    output = queries_f32 * inner_sum
    cot_f32 = out_cotangent.astype(jnp.float32)
    square_part = jnp.sum(output * output, axis=1)
    cross_part = jnp.sum(cot_f32 * output, axis=1)
    square_sum, cross_sum = lax.psum((square_part, cross_part), "dp")
    channels_all = channels * lax.axis_size("dp")
    rms = jnp.sqrt(square_sum / channels_all + 1e-05)
    cross_mean = cross_sum / channels_all
    token_scale = 1.0 / math.sqrt(local_rows * lax.axis_size("seq"))
    out_grad = (cot_f32 / rms[:, None] - output * (cross_mean / rms**3)[:, None]) * token_scale
    conv_grad = out_grad * queries_f32
    cotangent = conv_grad.astype(jnp.bfloat16)
    query_grad = out_grad * inner_sum
    cotangent_rim = shifted(cotangent[: filter_taps - 1], "seq", -1)
    backward_source = jnp.concatenate([cotangent, cotangent_rim], axis=0)
    product_grad = apply_band(long_filter, backward_source, block_rows) + skip_f32 * conv_grad
    all_grad = jnp.stack([query_grad, product_grad * value_f32, product_grad * key_f32])
    per_tap = []
    for tap_index in range(feat_taps):
        begin = feat_taps - 1 - tap_index
        per_tap.append(
            jnp.sum(
                all_grad * extended[:, begin : begin + local_rows, :].astype(jnp.float32), axis=1
            )
        )
    feat_grad = jnp.stack(per_tap)
    skip_grad = jnp.sum(conv_grad * product_f32, axis=0)
    filter_grad = filter_gradient(cotangent, forward_source, filter_taps, groups, block_rows)
    feat_out, filter_out, skip_out = lax.psum((feat_grad, filter_grad, skip_grad), "seq")
    return (feat_out, filter_out, skip_out)


def solution(mesh):
    return jax.shard_map(
        body,
        mesh=mesh,
        in_specs=(
            P(None, "seq", "dp"),
            P(None, None, "dp"),
            P("dp", None),
            P("dp"),
            P("seq", "dp"),
        ),
        out_specs=(P(None, None, "dp"), P("dp", None), P("dp")),
        check_vma=False,
    )
```

profile of v0, /device:TPU:1, one launch (start us, length us, event | category | flops | bytes accessed | tf_op | source)
XLA Modules:
  0.0 435.1 jit_solution(7712258792461225975)
XLA Ops:
  0.7 1.5 copy.10
  2.3 9.0 %collective-permute-start = (bf16[3,133,256]{1,2,0:T(8,128)(2,1)S(1)}, bf16[3,133,256]{1,2,0:T(8,128)(2,1)S(1)}, u32[]{:S(2)}, u32[]{:S(2)}) collective-permute-start(bf16[3,133,256]{1,2,0:T(8,128)(2,1)S(1)} %slice.198), channel_id=1, source_target_pairs={{0,16},{16,32},{32,48},{48,64},{64,80},{80,96},{96,112},{112,128},... | collective-permute-start | bytes 612872 | tf_op jit(solution)/shard_map/ppermute | solution.py:12
  11.8 7.1 %collective-permute-done = bf16[3,133,256]{1,2,0:T(8,128)(2,1)S(1)} collective-permute-done((bf16[3,133,256]{1,2,0:T(8,128)(2,1)S(1)}, bf16[3,133,256]{1,2,0:T(8,128)(2,1)S(1)}, u32[]{:S(2)}, u32[]{:S(2)}) %collective-permute-start) | collective-permute-done | bytes 204320 | tf_op jit(solution)/shard_map/ppermute | solution.py:12
  19.1 3.0 fusion.31
  24.4 20.5 %while.30 = (s32[]{:T(128)}, f32[4,2,256,4,16]{2,4,1,3,0:T(8,128)S(1)}, s32[4]{0:T(128)}, bf16[2,256,16,16]{1,3,0,2:T(8,128)(2,1)S(1)}, bf16[16,128]{1,0:T(8,128...) while((s32[]{:T(128)}, ...), condition=%wide.region_1.2_spmd, body=%wide.region_0.1_spmd.sunk | while | flops 25198596 | bytes 7308481 | solution.py:58
  27.3 1.7 reshape.95
  32.4 1.7 reshape.95
  37.6 1.7 reshape.95
  42.7 1.7 reshape.95
  45.6 28.8 %all-reduce.6 = (f32[512]{0:T(512)S(1)}, f32[512]{0:T(512)S(1)}) all-reduce(f32[512]{0:T(512)S(1)} %get-tuple-element.131, f32[512]{0:T(512)S(1)} %get-tuple-element.130), channel_id=1, replica_groups=mesh['seq'=64,'dp'=16] {'dp'}, use_global_device_ids=true, to_apply=%region_5.6 | all-reduce | flops 1024 | bytes 8192 | tf_op jit(solution)/shard_map/psum | solution.py:127
  74.4 1.7 fusion.48
  77.7 4.1 collective-permute-start.1
  81.8 36.3 %while.32 = (s32[]{:T(128)}, f32[4,4,128]{2,1,0:T(4,128)}, s32[4]{0:T(128)S(1)}, bf16[2,256,16,16]{1,3,0,2:T(8,128)(2,1)S(1)}, bf16[2,256,16,16]{1,3,0,2:T(8,128...) while((s32[]{:T(128)}, f32[4,4,128]{2,1,0:T(4,128)}, ...), condition=%wide.region_18.19_spmd, body=%wide.region_16.18_spmd.sunk | while | flops 25689604 | bytes 20173040 | solution.py:83
  85.8 3.5 reshape.97
  94.8 3.5 reshape.97
  103.9 3.5 reshape.97
  113.0 3.5 reshape.97
  120.4 18.0 %while.31 = (s32[]{:T(128)}, f32[4,2,256,4,16]{2,4,1,3,0:T(8,128)S(1)}, s32[4]{0:T(128)S(1)}, bf16[2,256,16,16]{1,3,0,2:T(8,128)(2,1)S(1)}, bf16[16,128]{1,0:T(8...) while((s32[]{:T(128)}, ...), condition=%wide.region_7.8_spmd, body=%wide.region_6.7_spmd.sunk | while | flops 25198596 | bytes 7371969 | solution.py:58
  122.6 1.7 reshape.96
  127.1 1.7 reshape.96
  131.6 1.7 reshape.96
  136.1 1.7 reshape.96
  140.2 3.2 fusion.37
  143.5 291.0 %all-reduce.5 = (f32[7,3,256]{2,1,0:T(4,128)S(1)}, f32[16,128]{1,0:T(8,128)}, f32[256]{0:T(256)}) all-reduce(f32[7,3,256]{2,1,0:T(4,128)S(1)} %constant_dynamic-update-slice_fusion, f32[16,128]{1,0:T(8,128)S(1)} %rev.9, f32[256]{0:T(256)S(1)} %copy-done.15), channel_id=1, replica_groups=mesh['seq'=64,'dp'=16] {'seq'}, use_global_device_ids=true, to_apply=%region_15.16 | all-reduce | flops 7680 | bytes 61440 | tf_op jit(solution)/shard_map/psum | solution.py:151
  (207 shorter events, 48.2 us)
Async XLA Ops:
  0.6 10.7 %copy-start.13 = (bf16[7,3,256]{2,0,1:T(8,128)(2,1)S(1)}, bf16[7,3,256]{2,0,1:T(8,128)(2,1)}, u32[]{:S(2)}) copy-start(bf16[7,3,256]{2,0,1:T(8,128)(2,1)} %param.12) | copy-start | bytes 32260
  0.6 10.8 %copy-start.14 = (bf16[16,128]{1,0:T(8,128)(2,1)S(1)}, bf16[16,128]{1,0:T(8,128)(2,1)}, u32[]{:S(2)}) copy-start(bf16[16,128]{1,0:T(8,128)(2,1)} %param.13) | copy-start | bytes 12292
  0.7 10.9 %copy-start.16 = (bf16[256]{0:T(256)(128)(2,1)S(1)}, bf16[256]{0:T(256)(128)(2,1)}, u32[]{:S(2)}) copy-start(bf16[256]{0:T(256)(128)(2,1)} %param.14) | copy-start | bytes 1540
  0.7 10.9 %copy-start.12 = (bf16[512,256]{1,0:T(8,128)(2,1)S(1)}, bf16[512,256]{1,0:T(8,128)(2,1)}, u32[]{:S(2)}) copy-start(bf16[512,256]{1,0:T(8,128)(2,1)} %param.15) | copy-start | bytes 786436
  2.1 19.9 %copy-start.2 = (bf16[3,512,256]{1,2,0:T(8,128)(2,1)}, bf16[3,512,256]{1,2,0:T(8,128)(2,1)S(1)}, u32[]{:S(2)}) copy-start(bf16[3,512,256]{1,2,0:T(8,128)(2,1)S(1)} %copy.10) | copy-start | bytes 2359300
  2.3 16.6 %collective-permute-start = (bf16[3,133,256]{1,2,0:T(8,128)(2,1)S(1)}, bf16[3,133,256]{1,2,0:T(8,128)(2,1)S(1)}, u32[]{:S(2)}, u32[]{:S(2)}) collective-permute-start(bf16[3,133,256]{1,2,0:T(8,128)(2,1)S(1)} %slice.198), channel_id=1, source_target_pairs={{0,16},{16,32},{32,48},{48,64},{64,80},{80,96},{96,112},{112,128},... | collective-permute-start | bytes 612872 | tf_op jit(solution)/shard_map/ppermute | solution.py:12
  19.1 3.8 copy-start.10
  22.1 52.3 %copy-start = (bf16[3,512,256]{1,2,0:T(8,128)(2,1)}, bf16[3,512,256]{1,2,0:T(8,128)(2,1)S(1)}, u32[]{:S(2)}) copy-start(bf16[3,512,256]{1,2,0:T(8,128)(2,1)S(1)} %fusion.31) | copy-start | bytes 2359300
  77.0 4.9 %copy-start.8 = (bf16[512,256]{0,1:T(8,128)(2,1)}, bf16[512,256]{0,1:T(8,128)(2,1)S(1)}, u32[]{:S(2)}) copy-start(bf16[512,256]{0,1:T(8,128)(2,1)S(1)} %convert_element_type.136) | copy-start | bytes 786436
  77.7 41.2 %collective-permute-start.1 = (bf16[127,256]{0,1:T(8,128)(2,1)}, bf16[127,256]{0,1:T(8,128)(2,1)}, u32[]{:S(2)}, u32[]{:S(2)}) collective-permute-start(bf16[127,256]{0,1:T(8,128)(2,1)} %slice.235), channel_id=1, source_target_pairs={{16,0},{32,16},{48,32},{64,48},{80,64},{96,80},{112,96},{128,112},... | collective-permute-start | bytes 195080 | tf_op jit(solution)/shard_map/ppermute | solution.py:12
  81.8 1.7 copy-start.6
  85.7 5.2 %copy-start.7 = (bf16[2,256,16,16]{1,3,0,2:T(8,128)(2,1)S(1)}, bf16[2,256,16,16]{1,3,0,2:T(8,128)(2,1)}, u32[]{:S(2)}) copy-start(bf16[2,256,16,16]{1,3,0,2:T(8,128)(2,1)} %copy-done.6) | copy-start | bytes 786436 | tf_op jit(solution)/shard_map/while
  90.9 1.7 copy-start.6
  94.8 5.2 %copy-start.7 = (bf16[2,256,16,16]{1,3,0,2:T(8,128)(2,1)S(1)}, bf16[2,256,16,16]{1,3,0,2:T(8,128)(2,1)}, u32[]{:S(2)}) copy-start(bf16[2,256,16,16]{1,3,0,2:T(8,128)(2,1)} %copy-done.6) | copy-start | bytes 786436 | tf_op jit(solution)/shard_map/while
  100.0 1.7 copy-start.6
  103.9 5.2 %copy-start.7 = (bf16[2,256,16,16]{1,3,0,2:T(8,128)(2,1)S(1)}, bf16[2,256,16,16]{1,3,0,2:T(8,128)(2,1)}, u32[]{:S(2)}) copy-start(bf16[2,256,16,16]{1,3,0,2:T(8,128)(2,1)} %copy-done.6) | copy-start | bytes 786436 | tf_op jit(solution)/shard_map/while
  109.1 1.7 copy-start.6
  113.0 5.2 %copy-start.7 = (bf16[2,256,16,16]{1,3,0,2:T(8,128)(2,1)S(1)}, bf16[2,256,16,16]{1,3,0,2:T(8,128)(2,1)}, u32[]{:S(2)}) copy-start(bf16[2,256,16,16]{1,3,0,2:T(8,128)(2,1)} %copy-done.6) | copy-start | bytes 786436 | tf_op jit(solution)/shard_map/while
  138.3 1.2 copy-start.1
  138.4 1.3 copy-start.5
  138.8 1.2 copy-start.3
  138.8 1.4 copy-start.9
  138.8 1.4 copy-start.11
  139.8 3.7 copy-start.15
  (1 other events, 0.8 us)
where the time goes:
time: 439 us; the launch traced here: 435 us
  blocking collectives  320 us (73%)
  local copies, waits for them, and re-layouts  64 us (15%)
  other arithmetic  15.3 us (3%)
  starting transfers between devices  13.1 us (3%)
  loops' own time  8.7 us (2%)
  waiting for transfers between devices  7.13 us (2%)
  matrix products  6 us (1%)
    psum x1, blocking collectives, body(): lax.psum((feat_grad, filter_grad, skip_grad), 'seq')  291 us
    psum x1, blocking collectives, body(): square_sum, cross_sum = lax.psum((square_part, cross_part), 'dp')  28.8 us
    reshape x4, local copies, waits for them, and re-layouts, filter_one_step(): diagonal = flat.reshape(step, block_rows, span + 1)[:, :, :filter_taps]  13.9 us
    reshape x8, local copies, waits for them, and re-layouts, band_matrix(): shaped = tiled.reshape(groups, block_rows, width)  13.8 us
    ppermute x2, starting transfers between devices, shifted(): return lax.ppermute(array, axis, pairs)  13.1 us
    dynamic_slice x12, local copies, waits for them, and re-layouts, apply_band(): pieces = lax.map(apply_one_step, jnp.arange(groups // step))  10.3 us
    while x36, local copies, waits for them, and re-layouts  9.55 us
  transfers between devices with their start and end apart: 2, of which 1 were waited for; matrix products, arithmetic and copies ran while one was open for 8% of the time, Pallas kernels for 0%

commit v1 on v0

v1 whole, which is shorter than its diff:
```python
import functools
import math

import jax
import jax.numpy as jnp
from jax import lax
from jax.experimental import pallas as pl
from jax.experimental.pallas import tpu as pltpu
from jax.sharding import PartitionSpec as P

F32 = jnp.float32
BF16 = jnp.bfloat16
LANES = 128
MEMBERS = 16
HALO = 144
MESH = pl.DeviceIdType.MESH


def iota(shape, dim):
    return lax.broadcasted_iota(jnp.int32, shape, dim)


def dot(lhs, rhs):
    return lax.dot_general(lhs, rhs, (((1,), (0,)), ((), ())), preferred_element_type=F32)


def dot_nt(lhs, rhs):
    return lax.dot_general(lhs, rhs, (((1,), (1,)), ((), ())), preferred_element_type=F32)


def aligned(index, step):
    return pl.multiple_of(index * step, step)


def fold(array):
    total = array[0:8]
    for begin in range(8, array.shape[0], 8):
        total = total + array[begin : begin + 8]
    return total


def kernel(geo, proj, taps, filt, skip, cot, out_f, out_l, out_s,
           pb, cb, tr, lf, sk, lff, wv, pf, kv, qv, xt, qt, gt, innt, ut, wt, inn, tof, tob, xg,
           pgt, skt, at, bt, st, acc, sla, slb, slc,
           ld_sem, h_s, h_r, s_s, s_r, a_s, a_r, b_s, b_r, c_s, c_r):
    n_seq, n_dp, n_y, n_z, rows, n_taps, channels = geo
    blocks = rows // LANES
    groups = channels // MEMBERS
    cts = channels // LANES
    me = lax.axis_index("seq")
    md = lax.axis_index("dp")
    my = me // n_z
    mz = lax.rem(me, n_z)
    mine = 64 // n_y

    loads = [
        pltpu.make_async_copy(filt, lf, ld_sem.at[0]),
        pltpu.make_async_copy(taps, tr, ld_sem.at[1]),
        pltpu.make_async_copy(skip, sk, ld_sem.at[2]),
        pltpu.make_async_copy(proj, pb.at[:, pl.ds(HALO, rows), :], ld_sem.at[3]),
        pltpu.make_async_copy(cot, cb, ld_sem.at[4]),
    ]
    for copy in loads:
        copy.start()

    barrier = pltpu.get_barrier_semaphore()

    def dp_peer(i):
        return {"dp": lax.rem(md + i, n_dp)}

    def y_index(i):
        return lax.rem(my + i, n_y)

    def y_peer(i):
        return {"seq": y_index(i) * n_z + mz}

    def z_peer(i):
        return {"seq": my * n_z + lax.rem(mz + i, n_z)}

    def greet(peer, count):
        @pl.loop(1, count)
        def _(i):
            pl.semaphore_signal(barrier, 1, device_id=peer(i), device_id_type=MESH)

    ahead = {"seq": lax.rem(me + 1, n_seq)}
    behind = {"seq": lax.rem(me + n_seq - 1, n_seq)}
    pl.semaphore_signal(barrier, 1, device_id=behind, device_id_type=MESH)
    pl.semaphore_signal(barrier, 1, device_id=ahead, device_id_type=MESH)
    greet(dp_peer, n_dp)
    greet(y_peer, n_y)
    greet(z_peer, n_z)

    for copy in loads[:3]:
        copy.wait()
    lff[...] = lf[...].astype(F32)
    for p in range(3):
        wv[p, 0:n_taps, :] = tr[p].astype(F32)
    row8 = iota((8, LANES), 0)
    keep = iota((LANES, LANES), 1) >= iota((LANES, LANES), 0)

    @pl.loop(0, groups)
    def _(g):
        base = jnp.broadcast_to(lff[pl.ds(g, 1), :], (8, LANES))
        for k in (1, 2, 4):
            base = jnp.where((row8 & k) != 0, pltpu.roll(base, k, 1), base)
        tiles = [base] + [pltpu.roll(base, 8 * r, 1) for r in range(1, LANES // 8)]
        circ = jnp.concatenate(tiles, axis=0)
        near = jnp.where(keep, circ, 0.0).astype(BF16)
        far = jnp.where(keep, 0.0, circ).astype(BF16)
        tof[g, 0:LANES, :] = far
        tof[g, LANES : 2 * LANES, :] = near
        tob[g, :, 0:LANES] = near
        tob[g, :, LANES : 2 * LANES] = far

    for ct in range(cts):
        cols = slice(ct * LANES, (ct + 1) * LANES)
        line = jnp.broadcast_to(sk[:, cols].astype(F32), (LANES, LANES))
        skt[cols, :] = line.T

    pl.semaphore_wait(barrier, n_dp + n_y + n_z - 1)
    halo = [
        pltpu.make_async_remote_copy(
            src_ref=proj.at[pl.ds(1, 2), pl.ds(rows - HALO, HALO), :],
            dst_ref=pb.at[pl.ds(1, 2), pl.ds(0, HALO), :],
            send_sem=h_s.at[0], recv_sem=h_r.at[0], device_id=ahead, device_id_type=MESH),
        pltpu.make_async_remote_copy(
            src_ref=proj.at[pl.ds(0, 1), pl.ds(rows - 16, 16), :],
            dst_ref=pb.at[pl.ds(0, 1), pl.ds(HALO - 16, 16), :],
            send_sem=h_s.at[1], recv_sem=h_r.at[1], device_id=ahead, device_id_type=MESH),
    ]

    @pl.when(me < n_seq - 1)
    def _():
        for copy in halo:
            copy.start()

    def featured(p, ct, block):
        window = pf.at[p * cts + ct, pl.ds(aligned(block, LANES), LANES + 16), :]
        total = None
        for j in range(n_taps):
            term = wv[p, j : j + 1, ct * LANES : (ct + 1) * LANES] * window[16 - j : 16 - j + LANES, :]
            total = term if total is None else total + term
        return total.astype(BF16).astype(F32)

    def widen(begin, count):
        for p in range(3):
            for ct in range(cts):
                pf[p * cts + ct, pl.ds(begin, count), :] = pb[
                    p, pl.ds(begin, count), ct * LANES : (ct + 1) * LANES].astype(F32)

    def product_block(block, with_query):
        for ct in range(cts):
            cols = slice(ct * LANES, (ct + 1) * LANES)
            here = pl.ds(aligned(block, LANES), LANES)
            keys = featured(1, ct, block)
            values = featured(2, ct, block)
            kv[ct, here, :] = keys
            kv[cts + ct, here, :] = values
            product = (keys * values).astype(BF16)
            xt[cols, here] = product.astype(F32).T.astype(BF16)
            if with_query:
                inside = pl.ds(aligned(block - 1, LANES), LANES)
                queries = featured(0, ct, block)
                qv[ct, inside, :] = queries
                qt[cols, inside] = queries.T
                gt[cols, inside] = cb[inside, cols].astype(F32).T

    loads[3].wait()

    @pl.loop(0, blocks)
    def _(block):
        widen(pl.multiple_of(HALO + block * LANES, 16), LANES)

    loads[4].wait()

    @pl.loop(2, blocks + 1)
    def _(block):
        product_block(block, True)

    @pl.when(me > 0)
    def _():
        for copy in halo:
            copy.wait_recv()

    @pl.when(me == 0)
    def _():
        pb[:, 0:HALO, :] = jnp.zeros((3, HALO, channels), BF16)

    widen(0, HALO)
    product_block(0, False)
    product_block(1, True)

    zero8 = jnp.zeros((8, LANES), F32)

    def forward(g, sums):
        sums = list(sums)
        r = pl.ds(aligned(g, MEMBERS), MEMBERS)
        source = [xt[r, b * LANES : (b + 1) * LANES] for b in range(blocks + 1)]
        left = jnp.concatenate(
            [jnp.concatenate([source[b], source[b + 1]], axis=1) for b in range(blocks)], axis=0)
        filtered = dot(left, tof[g])
        gain = skt[r, :]
        for b in range(blocks):
            cols = slice(b * LANES, (b + 1) * LANES)
            inner = filtered[b * MEMBERS : (b + 1) * MEMBERS] + gain * source[b + 1].astype(F32)
            queries = qt[r, cols]
            output = queries * inner
            cotangent = gt[r, cols]
            sums[b] = sums[b] + fold(output * output)
            sums[blocks + b] = sums[blocks + b] + fold(cotangent * output)
            innt[r, cols] = inner
            ut[r, cols] = cotangent * queries
            wt[r, cols] = output * queries
        return tuple(sums)

    sums = lax.fori_loop(0, groups, forward, (zero8,) * (2 * blocks), unroll=4)
    st[md] = jnp.concatenate([jnp.sum(part, axis=0, keepdims=True) for part in sums], axis=0)

    def stat_copy(i):
        return pltpu.make_async_remote_copy(
            src_ref=st.at[md], dst_ref=st.at[md], send_sem=s_s.at[i],
            recv_sem=s_r.at[md], device_id=dp_peer(i), device_id_type=MESH)

    @pl.loop(1, n_dp)
    def _(i):
        stat_copy(i).start()

    @pl.loop(0, blocks)
    def _(block):
        here = pl.ds(aligned(block, LANES), LANES)
        for ct in range(cts):
            inn[ct, here, :] = innt[ct * LANES : (ct + 1) * LANES, here].T

    @pl.loop(0, groups)
    def _(g):
        r = pl.ds(aligned(g, MEMBERS), MEMBERS)
        stack = [xt[r, b * LANES : (b + 1) * LANES].astype(F32) for b in range(blocks + 1)]
        stack.append(jnp.zeros((LANES - (blocks + 1) * MEMBERS, LANES), F32))
        xg[g] = jnp.concatenate(stack, axis=0).T.astype(BF16)

    @pl.loop(1, n_dp)
    def _(i):
        src = lax.rem(md + i, n_dp)
        pltpu.make_async_remote_copy(
            src_ref=st.at[src], dst_ref=st.at[src], send_sem=s_s.at[i],
            recv_sem=s_r.at[src], device_id=dp_peer(i), device_id_type=MESH).wait_recv()

    whole = st[0]
    for i in range(1, n_dp):
        whole = whole + st[i]
    mean = whole * (1.0 / (channels * n_dp))
    token_scale = 1.0 / math.sqrt(rows * n_seq)
    rms = jnp.sqrt(mean[0:blocks] + 1e-05)
    scale_a = token_scale / rms
    scale_b = token_scale * mean[blocks : 2 * blocks] / (rms * rms * rms)
    lines_a = [scale_a[b : b + 1] for b in range(blocks)]
    lines_b = [scale_b[b : b + 1] for b in range(blocks)]
    for b in range(blocks):
        at[b] = jnp.broadcast_to(lines_a[b], (LANES, LANES)).T
        bt[b] = jnp.broadcast_to(lines_b[b], (LANES, LANES)).T

    pad = jnp.zeros((MEMBERS, LANES), BF16)
    fill = jnp.zeros((LANES - (blocks + 1) * MEMBERS, LANES), BF16)

    def backward(g, carry):
        r = pl.ds(aligned(g, MEMBERS), MEMBERS)
        parts = []
        for b in range(blocks):
            cols = slice(b * LANES, (b + 1) * LANES)
            parts.append((ut[r, cols] * lines_a[b] - wt[r, cols] * lines_b[b]).astype(BF16))
        chain = [pad] + parts + [pad]
        left = jnp.concatenate(
            [jnp.concatenate([chain[b], chain[b + 1]], axis=1) for b in range(blocks + 1)], axis=0)
        grad = dot_nt(left, tob[g])
        for b in range(blocks + 1):
            pgt[r, b * LANES : (b + 1) * LANES] = grad[b * MEMBERS : (b + 1) * MEMBERS]
        right = jnp.concatenate(
            [jnp.concatenate(parts + [pad, fill], axis=0), jnp.concatenate([pad] + parts + [fill], axis=0)],
            axis=1)
        lagged = dot(xg[g], right)
        square = jnp.where(keep, lagged[:, LANES:], lagged[:, :LANES])
        total = square[0:8]
        for t in range(1, LANES // 8):
            total = total + pltpu.roll(square[8 * t : 8 * t + 8], LANES - 8 * t, 1)
        for k in (1, 2, 4):
            total = jnp.where((row8 & k) != 0, pltpu.roll(total, LANES - k, 1), total)
        acc[pl.ds(48 + g, 1), :] = jnp.sum(total, axis=0, keepdims=True)
        return carry

    lax.fori_loop(0, groups, backward, 0, unroll=2)

    for ct in range(cts):
        cols = slice(ct * LANES, (ct + 1) * LANES)
        gain = sk[:, cols].astype(F32)

        def taps_of(part, window, begin, count, grad, totals):
            for j in range(n_taps):
                term = grad * window[16 - j + begin : 16 - j + begin + count, :]
                totals[part * 8 + j] = totals[part * 8 + j] + fold(term)

        def tail(block, totals, inside):
            totals = list(totals)
            here = pl.ds(aligned(block, LANES), LANES)
            backed = pgt[cols, here].T
            windows = [
                pf.at[p * cts + ct, pl.ds(aligned(block, LANES), LANES + 16), :] for p in range(3)]
            step = 32
            for begin in range(0, LANES, step):
                local = pl.ds(pl.multiple_of(block * LANES + begin, 8), step)
                keys = kv[ct, local, :]
                values = kv[cts + ct, local, :]
                grad = backed[begin : begin + step]
                if inside:
                    own = pl.ds(pl.multiple_of((block - 1) * LANES + begin, 16), step)
                    queries = qv[ct, own, :]
                    inner = inn[ct, own, :]
                    first = at[block - 1, begin : begin + step, :]
                    second = bt[block - 1, begin : begin + step, :]
                    out_grad = cb[own, cols].astype(F32) * first - queries * inner * second
                    conv = out_grad * queries
                    grad = grad + gain * conv
                    product = (keys * values).astype(BF16).astype(F32)
                    totals[7] = totals[7] + fold(conv * product)
                    taps_of(0, windows[0], begin, step, out_grad * inner, totals)
                taps_of(1, windows[1], begin, step, grad * values, totals)
                taps_of(2, windows[2], begin, step, grad * keys, totals)
            return tuple(totals)

        totals = tail(0, (zero8,) * 24, False)
        totals = lax.fori_loop(1, blocks + 1, functools.partial(tail, inside=True), totals)
        for p in range(3):
            acc[(p * cts + ct) * 8 : (p * cts + ct) * 8 + 8, :] = jnp.concatenate(
                [jnp.sum(totals[p * 8 + j], axis=0, keepdims=True) for j in range(8)], axis=0)

    def a_copy(i):
        there = y_index(i)
        return pltpu.make_async_remote_copy(
            src_ref=acc.at[pl.ds(aligned(there, mine), mine), :], dst_ref=sla.at[my],
            send_sem=a_s.at[i], recv_sem=a_r.at[my], device_id=y_peer(i), device_id_type=MESH)

    def b_copy(i):
        return pltpu.make_async_remote_copy(
            src_ref=slb.at[mz], dst_ref=slb.at[mz],
            send_sem=b_s.at[i], recv_sem=b_r.at[mz], device_id=z_peer(i), device_id_type=MESH)

    def c_copy(i):
        return pltpu.make_async_remote_copy(
            src_ref=slc.at[my], dst_ref=slc.at[my],
            send_sem=c_s.at[i], recv_sem=c_r.at[my], device_id=y_peer(i), device_id_type=MESH)

    def arrived(slots, sends, receives, peer, index, i):
        src = index(i)
        pltpu.make_async_remote_copy(
            src_ref=slots.at[src], dst_ref=slots.at[src], send_sem=sends.at[i],
            recv_sem=receives.at[src], device_id=peer(i), device_id_type=MESH).wait_recv()

    def z_index(i):
        return lax.rem(mz + i, n_z)

    @pl.loop(1, n_y)
    def _(i):
        a_copy(i).start()

    sla[my] = acc[pl.ds(aligned(my, mine), mine), :]

    @pl.loop(1, n_y)
    def _(i):
        arrived(sla, a_s, a_r, y_peer, y_index, i)

    part = sla[0]
    for i in range(1, n_y):
        part = part + sla[i]
    slb[mz] = part

    @pl.loop(1, n_z)
    def _(i):
        b_copy(i).start()

    @pl.loop(1, n_z)
    def _(i):
        arrived(slb, b_s, b_r, z_peer, z_index, i)

    part = slb[0]
    for i in range(1, n_z):
        part = part + slb[i]
    slc[my] = part

    @pl.loop(1, n_y)
    def _(i):
        c_copy(i).start()

    @pl.loop(1, n_y)
    def _(i):
        arrived(slc, c_s, c_r, y_peer, y_index, i)

    def tile(number):
        begin = number * 8
        return slc[begin // mine, begin % mine : begin % mine + 8, :]

    for ct in range(cts):
        cols = slice(ct * LANES, (ct + 1) * LANES)
        for p in range(3):
            out_f[p, :, cols] = tile(p * cts + ct)[0:n_taps]
        out_s[:, cols] = tile(ct)[7:8]
    out_l[0:8, :] = tile(6)
    out_l[8:16, :] = tile(7)

    @pl.loop(1, n_dp)
    def _(i):
        stat_copy(i).wait_send()

    @pl.loop(1, n_y)
    def _(i):
        a_copy(i).wait_send()
        c_copy(i).wait_send()

    @pl.loop(1, n_z)
    def _(i):
        b_copy(i).wait_send()

    @pl.when(me < n_seq - 1)
    def _():
        for copy in halo:
            copy.wait_send()


def body(sizes, projected, featurizer, long_filter, skip_gain, out_cotangent):
    n_seq, n_dp = sizes
    parts, rows, channels = projected.shape
    n_taps = featurizer.shape[0]
    groups, filter_taps = long_filter.shape
    n_y = 1 << ((n_seq.bit_length() - 1) // 2)
    n_z = n_seq // n_y
    blocks = rows // LANES
    cts = channels // LANES
    mine = 64 // n_y
    geo = (n_seq, n_dp, n_y, n_z, rows, n_taps, channels)
    long = rows + LANES
    vmem = pltpu.VMEM
    dma = pltpu.SemaphoreType.DMA
    scratch = [
        vmem((3, HALO + rows, channels), BF16),
        vmem((rows, channels), BF16),
        vmem((3, n_taps, channels), BF16),
        vmem((groups, LANES), BF16),
        vmem((1, channels), BF16),
        vmem((groups, LANES), F32),
        vmem((3, 8, channels), F32),
        vmem((3 * cts, HALO + rows, LANES), F32),
        vmem((2 * cts, long, LANES), F32),
        vmem((cts, rows, LANES), F32),
        vmem((channels, long), BF16),
        vmem((channels, rows), F32),
        vmem((channels, rows), F32),
        vmem((channels, rows), F32),
        vmem((channels, rows), F32),
        vmem((channels, rows), F32),
        vmem((cts, rows, LANES), F32),
        vmem((groups, 2 * LANES, LANES), BF16),
        vmem((groups, LANES, 2 * LANES), BF16),
        vmem((groups, LANES, LANES), BF16),
        vmem((channels, long), F32),
        vmem((channels, LANES), F32),
        vmem((blocks, LANES, LANES), F32),
        vmem((blocks, LANES, LANES), F32),
        vmem((n_dp, 8, LANES), F32),
        vmem((64, LANES), F32),
        vmem((n_y, mine, LANES), F32),
        vmem((n_z, mine, LANES), F32),
        vmem((n_y, mine, LANES), F32),
        dma((5,)), dma((2,)), dma((2,)),
        dma((n_dp,)), dma((n_dp,)),
        dma((n_y,)), dma((n_y,)),
        dma((n_z,)), dma((n_z,)),
        dma((n_y,)), dma((n_y,)),
    ]
    anywhere = pl.BlockSpec(memory_space=pl.ANY)
    inside = pl.BlockSpec(memory_space=pltpu.VMEM)
    feat, filt, skip = pl.pallas_call(
        functools.partial(kernel, geo),
        out_shape=(
            jax.ShapeDtypeStruct((3, n_taps, channels), F32),
            jax.ShapeDtypeStruct((groups, filter_taps), F32),
            jax.ShapeDtypeStruct((1, channels), F32),
        ),
        in_specs=[anywhere] * 5,
        out_specs=(inside,) * 3,
        scratch_shapes=scratch,
        compiler_params=pltpu.CompilerParams(
            collective_id=0, has_side_effects=True, vmem_limit_bytes=48 * 1024 * 1024),
    )(projected, featurizer.transpose(1, 0, 2), long_filter, skip_gain.reshape(1, channels), out_cotangent)
    return feat.transpose(1, 0, 2), filt, skip.reshape(channels)


def solution(mesh):
    sizes = (mesh.shape["seq"], mesh.shape["dp"])
    return jax.shard_map(
        functools.partial(body, sizes),
        mesh=mesh,
        in_specs=(
            P(None, "seq", "dp"),
            P(None, None, "dp"),
            P("dp", None),
            P("dp"),
            P("seq", "dp"),
        ),
        out_specs=(P(None, None, "dp"), P("dp", None), P("dp")),
        check_vma=False,
    )
```

time: 439 us -> 62.3 us (0.14)
  blocking collectives: 320 us -> 0 us
  local copies, waits for them, and re-layouts: 64 us -> 5.9 us
  Pallas kernels: 0 us -> 55.4 us
  other arithmetic: 15.3 us -> 0 us
  starting transfers between devices: 13.1 us -> 0 us
  loops' own time: 8.7 us -> 0 us
  waiting for transfers between devices: 7.13 us -> 0 us
  matrix products: 6 us -> 0 us
    psum x2 -> x0, blocking collectives: 320 us -> none  [the longest x1 291 us: body(): lax.psum((feat_grad, filter_grad, skip_grad), 'seq')]
    pallas_call x0 -> x1, Pallas kernels: none -> 55.4 us  [body(): pl.pallas_call(functools.partial(kernel, geo), out_shape=(jax.ShapeDtypeS...]
    reshape x14 -> x1, local copies, waits for them, and re-layouts: 28.1 us -> 0.01 us  [body(): skip_gain.reshape(1, channels)]
    ppermute x2 -> x0, starting transfers between devices: 13.1 us -> none  [shifted(): return lax.ppermute(array, axis, pairs)]
    dynamic_slice x24 -> x0, local copies, waits for them, and re-layouts: 10.5 us -> none  [the longest x12 10.3 us: apply_band(): pieces = lax.map(apply_one_step, jnp.arange(groups // step))]
    while x39 -> x0, local copies, waits for them, and re-layouts: 9.62 us -> none
    reduce_sum x7 -> x0, other arithmetic: 9.5 us -> none  [the longest x4 4.36 us: filter_one_step(): return jnp.sum(diagonal, axis=1)]
    another operation x3 -> x0, loops' own time: 8.7 us -> none  [the longest x2 5.64 us: apply_band(): pieces = lax.map(apply_one_step, jnp.arange(groups // step))]
  transfers between devices with their start and end apart: 2 -> 0, of which waited for: 1 -> 0; matrix products, arithmetic and copies ran while one was open for 8% -> 0% of each run, Pallas kernels for 0% -> 0%
where the time goes in v1:
time: 62.3 us; the launch traced here: 62 us
  Pallas kernels  55.4 us (89%)
  local copies, waits for them, and re-layouts  5.9 us (9%)
  between operations  0.65 us (1%)
    pallas_call x1, Pallas kernels, body(): pl.pallas_call(functools.partial(kernel, geo), out_shape=(jax.ShapeDtypeS...  55.4 us
    unnamed x13, local copies, waits for them, and re-layouts  5.89 us

profile of v1, /device:TPU:1, one launch (start us, length us, event | category | flops | bytes accessed | tf_op | source)
XLA Modules:
  0.0 62.0 jit_solution(17358060106860836382)
XLA Ops:
  0.6 0.0 copy-start.4
  0.6 0.6 %copy-done.4 = bf16[256]{0:T(256)(128)(2,1)S(1)} copy-done((bf16[256]{0:T(256)(128)(2,1)S(1)}, bf16[256]{0:T(256)(128)(2,1)}, u32[]{:S(2)}) %copy-start.4) | copy-done | bytes 536
  1.3 0.0 copy-start
  1.3 1.1 %copy-done = bf16[3,512,256]{2,1,0:T(8,128)(2,1)S(1)} copy-done((bf16[3,512,256]{2,1,0:T(8,128)(2,1)S(1)}, bf16[3,512,256]{2,1,0:T(8,128)(2,1)}, u32[]{:S(2)}) %copy-start) | copy-done | bytes 786456
  2.4 0.0 copy-start.1
  2.4 0.9 %copy-done.1 = bf16[512,256]{1,0:T(8,128)(2,1)S(1)} copy-done((bf16[512,256]{1,0:T(8,128)(2,1)S(1)}, bf16[512,256]{1,0:T(8,128)(2,1)}, u32[]{:S(2)}) %copy-start.1) | copy-done | bytes 262168
  3.4 0.0 copy-start.2
  3.4 0.7 %copy-done.2 = bf16[7,3,256]{2,0,1:T(8,128)(2,1)S(1)} copy-done((bf16[7,3,256]{2,0,1:T(8,128)(2,1)S(1)}, bf16[7,3,256]{2,0,1:T(8,128)(2,1)}, u32[]{:S(2)}) %copy-start.2) | copy-done | bytes 10776
  4.1 0.0 copy-start.3
  4.1 0.7 %copy-done.3 = bf16[16,128]{1,0:T(8,128)(2,1)S(1)} copy-done((bf16[16,128]{1,0:T(8,128)(2,1)S(1)}, bf16[16,128]{1,0:T(8,128)(2,1)}, u32[]{:S(2)}) %copy-start.3) | copy-done | bytes 4120
  4.8 55.4 %shard_map.76 = (f32[3,7,256]{2,1,0:T(8,128)S(1)}, f32[16,128]{1,0:T(8,128)S(1)}, f32[1,256]{1,0:T(1,128)S(1)}) custom-call(bf16[3,512,256]{2,1,0:T(8,128)(2,1)S(1)} %copy-done, bf16[3,7,256]{2,1,0:T(8,128)(2,1)S(1)} %bitcast.4, bf16[16,128]{1,0:T(8,128)(2,1)S(1)} %copy-done.3, bf16[1,256]{1,0:T(2,128)(2,1)S(1)} %reshape.12.skip, bf16[512,256]{1,0:T(8,128)(2,1)S(1)} %copy-done.1), custom_call_target="tpu_custom_call" | custom-call | tf_op jit(solution)/shard_map/pallas_call | solution.py:479
  60.2 0.6 copy.11
  60.8 0.6 copy.12
  61.4 0.6 copy.13
  (1 shorter events, 0.0 us)
Async XLA Ops:
  0.6 0.7 %copy-start.4 = (bf16[256]{0:T(256)(128)(2,1)S(1)}, bf16[256]{0:T(256)(128)(2,1)}, u32[]{:S(2)}) copy-start(bf16[256]{0:T(256)(128)(2,1)} %param.8) | copy-start | bytes 1540
  1.3 1.1 %copy-start = (bf16[3,512,256]{2,1,0:T(8,128)(2,1)S(1)}, bf16[3,512,256]{2,1,0:T(8,128)(2,1)}, u32[]{:S(2)}) copy-start(bf16[3,512,256]{2,1,0:T(8,128)(2,1)} %proj.1) | copy-start | bytes 2359300
  2.4 0.9 %copy-start.1 = (bf16[512,256]{1,0:T(8,128)(2,1)S(1)}, bf16[512,256]{1,0:T(8,128)(2,1)}, u32[]{:S(2)}) copy-start(bf16[512,256]{1,0:T(8,128)(2,1)} %cot.1) | copy-start | bytes 786436
  3.4 0.7 %copy-start.2 = (bf16[7,3,256]{2,0,1:T(8,128)(2,1)S(1)}, bf16[7,3,256]{2,0,1:T(8,128)(2,1)}, u32[]{:S(2)}) copy-start(bf16[7,3,256]{2,0,1:T(8,128)(2,1)} %param.6) | copy-start | bytes 32260
  4.1 0.7 %copy-start.3 = (bf16[16,128]{1,0:T(8,128)(2,1)S(1)}, bf16[16,128]{1,0:T(8,128)(2,1)}, u32[]{:S(2)}) copy-start(bf16[16,128]{1,0:T(8,128)(2,1)} %filt.1) | copy-start | bytes 12292

commit v2 on v1

--- a/solution.py
+++ b/solution.py
@@ -41,7 +41,7 @@
 
 def kernel(geo, proj, taps, filt, skip, cot, out_f, out_l, out_s,
            pb, cb, tr, lf, sk, lff, wv, pf, kv, qv, xt, qt, gt, innt, ut, wt, inn, tof, tob, xg,
-           pgt, skt, at, bt, st, acc, sla, slb, slc,
+           pgt, skt, at, bt, st, acc, bases, slr, sly, slz,
            ld_sem, h_s, h_r, s_s, s_r, a_s, a_r, b_s, b_r, c_s, c_r):
     n_seq, n_dp, n_y, n_z, rows, n_taps, channels = geo
     blocks = rows // LANES
@@ -51,7 +51,8 @@
     md = lax.axis_index("dp")
     my = me // n_z
     mz = lax.rem(me, n_z)
-    mine = 64 // n_y
+    core = lax.rem(mz, 2)
+    half = 32
 
     loads = [
         pltpu.make_async_copy(filt, lf, ld_sem.at[0]),
@@ -92,47 +93,8 @@
 
     for copy in loads[:3]:
         copy.wait()
-    lff[...] = lf[...].astype(F32)
     for p in range(3):
         wv[p, 0:n_taps, :] = tr[p].astype(F32)
-    row8 = iota((8, LANES), 0)
-    keep = iota((LANES, LANES), 1) >= iota((LANES, LANES), 0)
-
-    @pl.loop(0, groups)
-    def _(g):
-        base = jnp.broadcast_to(lff[pl.ds(g, 1), :], (8, LANES))
-        for k in (1, 2, 4):
-            base = jnp.where((row8 & k) != 0, pltpu.roll(base, k, 1), base)
-        tiles = [base] + [pltpu.roll(base, 8 * r, 1) for r in range(1, LANES // 8)]
-        circ = jnp.concatenate(tiles, axis=0)
-        near = jnp.where(keep, circ, 0.0).astype(BF16)
-        far = jnp.where(keep, 0.0, circ).astype(BF16)
-        tof[g, 0:LANES, :] = far
-        tof[g, LANES : 2 * LANES, :] = near
-        tob[g, :, 0:LANES] = near
-        tob[g, :, LANES : 2 * LANES] = far
-
-    for ct in range(cts):
-        cols = slice(ct * LANES, (ct + 1) * LANES)
-        line = jnp.broadcast_to(sk[:, cols].astype(F32), (LANES, LANES))
-        skt[cols, :] = line.T
-
-    pl.semaphore_wait(barrier, n_dp + n_y + n_z - 1)
-    halo = [
-        pltpu.make_async_remote_copy(
-            src_ref=proj.at[pl.ds(1, 2), pl.ds(rows - HALO, HALO), :],
-            dst_ref=pb.at[pl.ds(1, 2), pl.ds(0, HALO), :],
-            send_sem=h_s.at[0], recv_sem=h_r.at[0], device_id=ahead, device_id_type=MESH),
-        pltpu.make_async_remote_copy(
-            src_ref=proj.at[pl.ds(0, 1), pl.ds(rows - 16, 16), :],
-            dst_ref=pb.at[pl.ds(0, 1), pl.ds(HALO - 16, 16), :],
-            send_sem=h_s.at[1], recv_sem=h_r.at[1], device_id=ahead, device_id_type=MESH),
-    ]
-
-    @pl.when(me < n_seq - 1)
-    def _():
-        for copy in halo:
-            copy.start()
 
     def featured(p, ct, block):
         window = pf.at[p * cts + ct, pl.ds(aligned(block, LANES), LANES + 16), :]
@@ -148,7 +110,7 @@
                 pf[p * cts + ct, pl.ds(begin, count), :] = pb[
                     p, pl.ds(begin, count), ct * LANES : (ct + 1) * LANES].astype(F32)
 
-    def product_block(block, with_query):
+    def product_block(block):
         for ct in range(cts):
             cols = slice(ct * LANES, (ct + 1) * LANES)
             here = pl.ds(aligned(block, LANES), LANES)
@@ -158,12 +120,15 @@
             kv[cts + ct, here, :] = values
             product = (keys * values).astype(BF16)
             xt[cols, here] = product.astype(F32).T.astype(BF16)
-            if with_query:
-                inside = pl.ds(aligned(block - 1, LANES), LANES)
-                queries = featured(0, ct, block)
-                qv[ct, inside, :] = queries
-                qt[cols, inside] = queries.T
-                gt[cols, inside] = cb[inside, cols].astype(F32).T
+
+    def query_block(block):
+        for ct in range(cts):
+            cols = slice(ct * LANES, (ct + 1) * LANES)
+            inside = pl.ds(aligned(block - 1, LANES), LANES)
+            queries = featured(0, ct, block)
+            qv[ct, inside, :] = queries
+            qt[cols, inside] = queries.T
+            gt[cols, inside] = cb[inside, cols].astype(F32).T
 
     loads[3].wait()
 
@@ -171,24 +136,82 @@
     def _(block):
         widen(pl.multiple_of(HALO + block * LANES, 16), LANES)
 
+    product_block(blocks)
+
+    pl.semaphore_wait(barrier, n_dp + n_y + n_z - 1)
+
+    def rim(number, src, dst):
+        return pltpu.make_async_remote_copy(
+            src_ref=src, dst_ref=dst, send_sem=h_s.at[number], recv_sem=h_r.at[number],
+            device_id=ahead, device_id_type=MESH)
+
+    halo = [
+        rim(0, proj.at[:, pl.ds(rows - 16, 16), :], pb.at[:, pl.ds(HALO - 16, 16), :]),
+        rim(1, xt.at[:, pl.ds(rows, LANES)], xt.at[:, pl.ds(0, LANES)]),
+        rim(2, proj.at[pl.ds(1, 2), pl.ds(rows - HALO, LANES), :],
+            pb.at[pl.ds(1, 2), pl.ds(0, LANES), :]),
+    ]
+
+    @pl.when(me < n_seq - 1)
+    def _():
+        for copy in halo:
+            copy.start()
+
     loads[4].wait()
+
+    @pl.loop(2, blocks)
+    def _(block):
+        product_block(block)
 
     @pl.loop(2, blocks + 1)
     def _(block):
-        product_block(block, True)
+        query_block(block)
+
+    lff[...] = lf[...].astype(F32)
+    row8 = iota((8, LANES), 0)
+    row_all = iota((8 * groups, LANES), 0)
+    keep = iota((LANES, LANES), 1) >= iota((LANES, LANES), 0)
+    base = jnp.concatenate(
+        [jnp.broadcast_to(lff[g : g + 1, :], (8, LANES)) for g in range(groups)], axis=0)
+    for k in (1, 2, 4):
+        base = jnp.where((row_all & k) != 0, pltpu.roll(base, k, 1), base)
+    bases[...] = base
+
+    def toeplitz(g, carry):
+        base = bases[pl.ds(aligned(g, 8), 8), :]
+        tiles = [base] + [pltpu.roll(base, 8 * r, 1) for r in range(1, LANES // 8)]
+        circ = jnp.concatenate(tiles, axis=0)
+        near = jnp.where(keep, circ, 0.0).astype(BF16)
+        far = jnp.where(keep, 0.0, circ).astype(BF16)
+        tof[g, 0:LANES, :] = far
+        tof[g, LANES : 2 * LANES, :] = near
+        tob[g, :, 0:LANES] = near
+        tob[g, :, LANES : 2 * LANES] = far
+        return carry
+
+    lax.fori_loop(0, groups, toeplitz, 0, unroll=4)
+
+    for ct in range(cts):
+        cols = slice(ct * LANES, (ct + 1) * LANES)
+        line = jnp.broadcast_to(sk[ct : ct + 1, :].astype(F32), (LANES, LANES))
+        skt[cols, :] = line.T
 
     @pl.when(me > 0)
     def _():
-        for copy in halo:
-            copy.wait_recv()
+        halo[0].wait_recv()
 
     @pl.when(me == 0)
     def _():
         pb[:, 0:HALO, :] = jnp.zeros((3, HALO, channels), BF16)
-
-    widen(0, HALO)
-    product_block(0, False)
-    product_block(1, True)
+        xt[:, 0:LANES] = jnp.zeros((channels, LANES), BF16)
+
+    widen(HALO - 16, 16)
+    product_block(1)
+    query_block(1)
+
+    @pl.when(me > 0)
+    def _():
+        halo[1].wait_recv()
 
     zero8 = jnp.zeros((8, LANES), F32)
 
@@ -238,6 +261,15 @@
         stack.append(jnp.zeros((LANES - (blocks + 1) * MEMBERS, LANES), F32))
         xg[g] = jnp.concatenate(stack, axis=0).T.astype(BF16)
 
+    @pl.when(me > 0)
+    def _():
+        halo[2].wait_recv()
+
+    widen(0, LANES)
+    for ct in range(cts):
+        for p in (1, 2):
+            kv[(p - 1) * cts + ct, 0:LANES, :] = featured(p, ct, 0)
+
     @pl.loop(1, n_dp)
     def _(i):
         src = lax.rem(md + i, n_dp)
@@ -282,16 +314,19 @@
         total = square[0:8]
         for t in range(1, LANES // 8):
             total = total + pltpu.roll(square[8 * t : 8 * t + 8], LANES - 8 * t, 1)
-        for k in (1, 2, 4):
-            total = jnp.where((row8 & k) != 0, pltpu.roll(total, LANES - k, 1), total)
-        acc[pl.ds(48 + g, 1), :] = jnp.sum(total, axis=0, keepdims=True)
+        bases[pl.ds(aligned(g, 8), 8), :] = total
         return carry
 
-    lax.fori_loop(0, groups, backward, 0, unroll=2)
+    lax.fori_loop(0, groups, backward, 0, unroll=4)
+    lag = bases[...]
+    for k in (1, 2, 4):
+        lag = jnp.where((row_all & k) != 0, pltpu.roll(lag, LANES - k, 1), lag)
+    acc[48 : 48 + groups, :] = jnp.concatenate(
+        [jnp.sum(lag[8 * g : 8 * g + 8], axis=0, keepdims=True) for g in range(groups)], axis=0)
 
     for ct in range(cts):
         cols = slice(ct * LANES, (ct + 1) * LANES)
-        gain = sk[:, cols].astype(F32)
+        gain = sk[ct : ct + 1, :].astype(F32)
 
         def taps_of(part, window, begin, count, grad, totals):
             for j in range(n_taps):
@@ -332,70 +367,53 @@
             acc[(p * cts + ct) * 8 : (p * cts + ct) * 8 + 8, :] = jnp.concatenate(
                 [jnp.sum(totals[p * 8 + j], axis=0, keepdims=True) for j in range(8)], axis=0)
 
-    def a_copy(i):
-        there = y_index(i)
-        return pltpu.make_async_remote_copy(
-            src_ref=acc.at[pl.ds(aligned(there, mine), mine), :], dst_ref=sla.at[my],
-            send_sem=a_s.at[i], recv_sem=a_r.at[my], device_id=y_peer(i), device_id_type=MESH)
-
-    def b_copy(i):
-        return pltpu.make_async_remote_copy(
-            src_ref=slb.at[mz], dst_ref=slb.at[mz],
-            send_sem=b_s.at[i], recv_sem=b_r.at[mz], device_id=z_peer(i), device_id_type=MESH)
-
-    def c_copy(i):
-        return pltpu.make_async_remote_copy(
-            src_ref=slc.at[my], dst_ref=slc.at[my],
-            send_sem=c_s.at[i], recv_sem=c_r.at[my], device_id=y_peer(i), device_id_type=MESH)
-
-    def arrived(slots, sends, receives, peer, index, i):
-        src = index(i)
-        pltpu.make_async_remote_copy(
-            src_ref=slots.at[src], dst_ref=slots.at[src], send_sem=sends.at[i],
-            recv_sem=receives.at[src], device_id=peer(i), device_id_type=MESH).wait_recv()
+    partner = {"seq": me + 1 - 2 * core}
+    swap = pltpu.make_async_remote_copy(
+        src_ref=acc.at[pl.ds(aligned(1 - core, half), half), :], dst_ref=slr,
+        send_sem=a_s.at[0], recv_sem=a_r.at[0], device_id=partner, device_id_type=MESH)
+    swap.start()
 
     def z_index(i):
         return lax.rem(mz + i, n_z)
 
+    def exchange(slots, sends, receives, place, i, peer):
+        return pltpu.make_async_remote_copy(
+            src_ref=slots.at[place], dst_ref=slots.at[place], send_sem=sends.at[i],
+            recv_sem=receives.at[place], device_id=peer(i), device_id_type=MESH)
+
+    swap.wait_recv()
+    sly[my] = (acc[pl.ds(aligned(core, half), half), :] + slr[...]).astype(BF16)
+
     @pl.loop(1, n_y)
     def _(i):
-        a_copy(i).start()
-
-    sla[my] = acc[pl.ds(aligned(my, mine), mine), :]
+        exchange(sly, b_s, b_r, my, i, y_peer).start()
 
     @pl.loop(1, n_y)
     def _(i):
-        arrived(sla, a_s, a_r, y_peer, y_index, i)
-
-    part = sla[0]
+        exchange(sly, b_s, b_r, y_index(i), i, y_peer).wait_recv()
+
+    part = sly[0].astype(F32)
     for i in range(1, n_y):
-        part = part + sla[i]
-    slb[mz] = part
+        part = part + sly[i].astype(F32)
+    slz[mz] = part.astype(BF16)
 
     @pl.loop(1, n_z)
     def _(i):
-        b_copy(i).start()
+        exchange(slz, c_s, c_r, mz, i, z_peer).start()
 
     @pl.loop(1, n_z)
     def _(i):
-        arrived(slb, b_s, b_r, z_peer, z_index, i)
-
-    part = slb[0]
-    for i in range(1, n_z):
-        part = part + slb[i]
-    slc[my] = part
-
-    @pl.loop(1, n_y)
-    def _(i):
-        c_copy(i).start()
-
-    @pl.loop(1, n_y)
-    def _(i):
-        arrived(slc, c_s, c_r, y_peer, y_index, i)
+        exchange(slz, c_s, c_r, z_index(i), i, z_peer).wait_recv()
+
+    halves = []
+    for h in range(2):
+        part = slz[h].astype(F32)
+        for i in range(1, n_z // 2):
+            part = part + slz[2 * i + h].astype(F32)
+        halves.append(part)
 
     def tile(number):
-        begin = number * 8
-        return slc[begin // mine, begin % mine : begin % mine + 8, :]
+        return halves[number // 4][number % 4 * 8 : number % 4 * 8 + 8]
 
     for ct in range(cts):
         cols = slice(ct * LANES, (ct + 1) * LANES)
@@ -409,14 +427,15 @@
     def _(i):
         stat_copy(i).wait_send()
 
+    swap.wait_send()
+
     @pl.loop(1, n_y)
     def _(i):
-        a_copy(i).wait_send()
-        c_copy(i).wait_send()
+        exchange(sly, b_s, b_r, my, i, y_peer).wait_send()
 
     @pl.loop(1, n_z)
     def _(i):
-        b_copy(i).wait_send()
+        exchange(slz, c_s, c_r, mz, i, z_peer).wait_send()
 
     @pl.when(me < n_seq - 1)
     def _():
@@ -433,7 +452,6 @@
     n_z = n_seq // n_y
     blocks = rows // LANES
     cts = channels // LANES
-    mine = 64 // n_y
     geo = (n_seq, n_dp, n_y, n_z, rows, n_taps, channels)
     long = rows + LANES
     vmem = pltpu.VMEM
@@ -443,7 +461,7 @@
         vmem((rows, channels), BF16),
         vmem((3, n_taps, channels), BF16),
         vmem((groups, LANES), BF16),
-        vmem((1, channels), BF16),
+        vmem((cts, LANES), BF16),
         vmem((groups, LANES), F32),
         vmem((3, 8, channels), F32),
         vmem((3 * cts, HALO + rows, LANES), F32),
@@ -465,14 +483,15 @@
         vmem((blocks, LANES, LANES), F32),
         vmem((n_dp, 8, LANES), F32),
         vmem((64, LANES), F32),
-        vmem((n_y, mine, LANES), F32),
-        vmem((n_z, mine, LANES), F32),
-        vmem((n_y, mine, LANES), F32),
-        dma((5,)), dma((2,)), dma((2,)),
+        vmem((8 * groups, LANES), F32),
+        vmem((32, LANES), F32),
+        vmem((n_y, 32, LANES), BF16),
+        vmem((n_z, 32, LANES), BF16),
+        dma((5,)), dma((3,)), dma((3,)),
         dma((n_dp,)), dma((n_dp,)),
+        dma((1,)), dma((1,)),
         dma((n_y,)), dma((n_y,)),
         dma((n_z,)), dma((n_z,)),
-        dma((n_y,)), dma((n_y,)),
     ]
     anywhere = pl.BlockSpec(memory_space=pl.ANY)
     inside = pl.BlockSpec(memory_space=pltpu.VMEM)
@@ -487,8 +506,8 @@
         out_specs=(inside,) * 3,
         scratch_shapes=scratch,
         compiler_params=pltpu.CompilerParams(
-            collective_id=0, has_side_effects=True, vmem_limit_bytes=48 * 1024 * 1024),
-    )(projected, featurizer.transpose(1, 0, 2), long_filter, skip_gain.reshape(1, channels), out_cotangent)
+            collective_id=0, has_side_effects=True, vmem_limit_bytes=60 * 1024 * 1024),
+    )(projected, featurizer.transpose(1, 0, 2), long_filter, skip_gain.reshape(cts, LANES), out_cotangent)
     return feat.transpose(1, 0, 2), filt, skip.reshape(channels)
 
 

time: 62.3 us -> 55.6 us (0.89)
  local copies, waits for them, and re-layouts: 5.9 us -> 2.58 us
  Pallas kernels: 55.4 us -> 52.1 us
    pallas_call x1, Pallas kernels: 55.4 us -> 52.1 us  [body(): pl.pallas_call(functools.partial(kernel, geo), out_shape=(jax.ShapeDtypeS...]
    unnamed x13 -> x7, local copies, waits for them, and re-layouts: 5.89 us -> 2.58 us
where the time goes in v2:
time: 55.6 us; the launch traced here: 55.3 us
  Pallas kernels  52.1 us (94%)
  local copies, waits for them, and re-layouts  2.58 us (5%)
  between operations  0.65 us (1%)
    pallas_call x1, Pallas kernels, body(): pl.pallas_call(functools.partial(kernel, geo), out_shape=(jax.ShapeDtypeS...  52.1 us
    unnamed x7, local copies, waits for them, and re-layouts  2.58 us

profile of v2, /device:TPU:1, one launch (start us, length us, event | category | flops | bytes accessed | tf_op | source)
XLA Modules:
  0.0 55.3 jit_solution(6680729126404376107)
XLA Ops:
  0.6 52.1 %shard_map.76 = (f32[3,7,256]{2,1,0:T(8,128)}, f32[16,128]{1,0:T(8,128)}, f32[1,256]{1,0:T(1,128)}) custom-call(bf16[3,512,256]{2,1,0:T(8,128)(2,1)} %proj.1, bf16[3,7,256]{2,1,0:T(8,128)(2,1)} %bitcast.5, bf16[16,128]{1,0:T(8,128)(2,1)} %filt.1, bf16[2,128]{1,0:T(2,128)(2,1)} %bitcast.7, bf16[512,256]{1,0:T(8,128)(2,1)} %cot.1), custom_call_target="tpu_custom_call" | custom-call | tf_op jit(solution)/shard_map/pallas_call | solution.py:498
  52.7 0.0 copy-start
  52.7 1.4 %copy.11 = f32[7,3,256]{2,0,1:T(8,128)} copy(f32[7,3,256]{2,0,1:T(8,128)} %bitcast.4) | data formatting | bytes 43008
  54.1 0.0 copy-done
  54.1 0.0 copy-start.1
  54.1 0.6 %copy.12 = f32[16,128]{1,0:T(8,128)} copy(f32[16,128]{1,0:T(8,128)S(1)} %copy-done) | data formatting | bytes 16384
  54.7 0.1 copy-done.1
  54.8 0.6 %copy.13 = f32[256]{0:T(256)} copy(f32[256]{0:T(256)S(1)} %bitcast.6) | data formatting | bytes 2048
Async XLA Ops:
  52.7 1.4 %copy-start = (f32[16,128]{1,0:T(8,128)S(1)}, f32[16,128]{1,0:T(8,128)}, u32[]{:S(2)}) copy-start(f32[16,128]{1,0:T(8,128)} %get-tuple-element.13) | copy-start | bytes 24580
  54.1 0.7 %copy-start.1 = (f32[1,256]{1,0:T(1,128)S(1)}, f32[1,256]{1,0:T(1,128)}, u32[]{:S(2)}) copy-start(f32[1,256]{1,0:T(1,128)} %get-tuple-element.8) | copy-start | bytes 3076

commit v3 on v2

--- a/solution.py
+++ b/solution.py
@@ -39,7 +39,7 @@
     return total
 
 
-def kernel(geo, proj, taps, filt, skip, cot, out_f, out_l, out_s,
+def kernel(geo, proj, taps, filt, skip, cot, out,
            pb, cb, tr, lf, sk, lff, wv, pf, kv, qv, xt, qt, gt, innt, ut, wt, inn, tof, tob, xg,
            pgt, skt, at, bt, st, acc, bases, slr, sly, slz,
            ld_sem, h_s, h_r, s_s, s_r, a_s, a_r, b_s, b_r, c_s, c_r):
@@ -61,9 +61,6 @@
         pltpu.make_async_copy(proj, pb.at[:, pl.ds(HALO, rows), :], ld_sem.at[3]),
         pltpu.make_async_copy(cot, cb, ld_sem.at[4]),
     ]
-    for copy in loads:
-        copy.start()
-
     barrier = pltpu.get_barrier_semaphore()
 
     def dp_peer(i):
@@ -87,6 +84,8 @@
     behind = {"seq": lax.rem(me + n_seq - 1, n_seq)}
     pl.semaphore_signal(barrier, 1, device_id=behind, device_id_type=MESH)
     pl.semaphore_signal(barrier, 1, device_id=ahead, device_id_type=MESH)
+    for copy in loads:
+        copy.start()
     greet(dp_peer, n_dp)
     greet(y_peer, n_y)
     greet(z_peer, n_z)
@@ -154,8 +153,8 @@
 
     @pl.when(me < n_seq - 1)
     def _():
-        for copy in halo:
-            copy.start()
+        halo[0].start()
+        halo[1].start()
 
     loads[4].wait()
 
@@ -208,6 +207,10 @@
     widen(HALO - 16, 16)
     product_block(1)
     query_block(1)
+
+    @pl.when(me < n_seq - 1)
+    def _():
+        halo[2].start()
 
     @pl.when(me > 0)
     def _():
@@ -236,7 +239,7 @@
             wt[r, cols] = output * queries
         return tuple(sums)
 
-    sums = lax.fori_loop(0, groups, forward, (zero8,) * (2 * blocks), unroll=4)
+    sums = lax.fori_loop(0, groups, forward, (zero8,) * (2 * blocks), unroll=8)
     st[md] = jnp.concatenate([jnp.sum(part, axis=0, keepdims=True) for part in sums], axis=0)
 
     def stat_copy(i):
@@ -317,7 +320,7 @@
         bases[pl.ds(aligned(g, 8), 8), :] = total
         return carry
 
-    lax.fori_loop(0, groups, backward, 0, unroll=4)
+    lax.fori_loop(0, groups, backward, 0, unroll=8)
     lag = bases[...]
     for k in (1, 2, 4):
         lag = jnp.where((row_all & k) != 0, pltpu.roll(lag, LANES - k, 1), lag)
@@ -405,42 +408,42 @@
     def _(i):
         exchange(slz, c_s, c_r, z_index(i), i, z_peer).wait_recv()
 
-    halves = []
     for h in range(2):
         part = slz[h].astype(F32)
         for i in range(1, n_z // 2):
             part = part + slz[2 * i + h].astype(F32)
-        halves.append(part)
-
-    def tile(number):
-        return halves[number // 4][number % 4 * 8 : number % 4 * 8 + 8]
-
+        out[h * half : (h + 1) * half, :] = part
+
+    @pl.loop(1, n_dp)
+    def _(i):
+        stat_copy(i).wait_send()
+
+    swap.wait_send()
+
+    @pl.loop(1, n_y)
+    def _(i):
+        exchange(sly, b_s, b_r, my, i, y_peer).wait_send()
+
+    @pl.loop(1, n_z)
+    def _(i):
+        exchange(slz, c_s, c_r, mz, i, z_peer).wait_send()
+
+    @pl.when(me < n_seq - 1)
+    def _():
+        for copy in halo:
+            copy.wait_send()
+
+
+def unpack(packed, out_f, out_l, out_s):
+    parts, n_taps, channels = out_f.shape
+    cts = channels // LANES
     for ct in range(cts):
         cols = slice(ct * LANES, (ct + 1) * LANES)
-        for p in range(3):
-            out_f[p, :, cols] = tile(p * cts + ct)[0:n_taps]
-        out_s[:, cols] = tile(ct)[7:8]
-    out_l[0:8, :] = tile(6)
-    out_l[8:16, :] = tile(7)
-
-    @pl.loop(1, n_dp)
-    def _(i):
-        stat_copy(i).wait_send()
-
-    swap.wait_send()
-
-    @pl.loop(1, n_y)
-    def _(i):
-        exchange(sly, b_s, b_r, my, i, y_peer).wait_send()
-
-    @pl.loop(1, n_z)
-    def _(i):
-        exchange(slz, c_s, c_r, mz, i, z_peer).wait_send()
-
-    @pl.when(me < n_seq - 1)
-    def _():
-        for copy in halo:
-            copy.wait_send()
+        for p in range(parts):
+            begin = (p * cts + ct) * 8
+            out_f[p, :, cols] = packed[begin : begin + n_taps, :]
+        out_s[:, cols] = packed[ct * 8 + 7 : ct * 8 + 8, :]
+    out_l[...] = packed[parts * cts * 8 :, :]
 
 
 def body(sizes, projected, featurizer, long_filter, skip_gain, out_cotangent):
@@ -493,21 +496,27 @@
         dma((n_y,)), dma((n_y,)),
         dma((n_z,)), dma((n_z,)),
     ]
-    anywhere = pl.BlockSpec(memory_space=pl.ANY)
     inside = pl.BlockSpec(memory_space=pltpu.VMEM)
-    feat, filt, skip = pl.pallas_call(
+    packed = pl.pallas_call(
         functools.partial(kernel, geo),
-        out_shape=(
-            jax.ShapeDtypeStruct((3, n_taps, channels), F32),
-            jax.ShapeDtypeStruct((groups, filter_taps), F32),
-            jax.ShapeDtypeStruct((1, channels), F32),
-        ),
-        in_specs=[anywhere] * 5,
-        out_specs=(inside,) * 3,
+        out_shape=jax.ShapeDtypeStruct((64, LANES), F32),
+        in_specs=[pl.BlockSpec(memory_space=pltpu.HBM)] * 5,
+        out_specs=inside,
         scratch_shapes=scratch,
         compiler_params=pltpu.CompilerParams(
             collective_id=0, has_side_effects=True, vmem_limit_bytes=60 * 1024 * 1024),
     )(projected, featurizer.transpose(1, 0, 2), long_filter, skip_gain.reshape(cts, LANES), out_cotangent)
+    feat, filt, skip = pl.pallas_call(
+        unpack,
+        out_shape=(
+            jax.ShapeDtypeStruct((parts, n_taps, channels), F32),
+            jax.ShapeDtypeStruct((groups, filter_taps), F32),
+            jax.ShapeDtypeStruct((1, channels), F32),
+        ),
+        in_specs=[inside],
+        out_specs=(inside,) * 3,
+        compiler_params=pltpu.CompilerParams(vmem_limit_bytes=60 * 1024 * 1024),
+    )(packed)
     return feat.transpose(1, 0, 2), filt, skip.reshape(channels)
 
 

time: 55.6 us -> 52.2 us (0.939)
  local copies, waits for them, and re-layouts: 2.58 us -> 0 us
  Pallas kernels: 52.1 us -> 51.4 us
    unnamed x7 -> x0, local copies, waits for them, and re-layouts: 2.58 us -> none
    pallas_call x1 -> x2, Pallas kernels: 52.1 us -> 51.4 us  [the longest x1 50 us: body(): pl.pallas_call(functools.partial(kernel, geo), out_shape=jax.ShapeDtypeSt...]
where the time goes in v3:
time: 52.2 us; the launch traced here: 52 us
  Pallas kernels  51.4 us (98%)
  between operations  0.64 us (1%)
    pallas_call x1, Pallas kernels, body(): pl.pallas_call(functools.partial(kernel, geo), out_shape=jax.ShapeDtypeSt...  50 us
    pallas_call x1, Pallas kernels, body(): pl.pallas_call(unpack, out_shape=(jax.ShapeDtypeStruct((parts, n_taps, ch...  1.38 us

profile of v3, /device:TPU:1, one launch (start us, length us, event | category | flops | bytes accessed | tf_op | source)
XLA Modules:
  0.0 52.0 jit_solution(17693132449928095021)
XLA Ops:
  0.6 50.0 %shard_map.76.packed = f32[64,128]{1,0:T(8,128)} custom-call(bf16[3,512,256]{2,1,0:T(8,128)(2,1)} %proj.1, bf16[3,7,256]{2,1,0:T(8,128)(2,1)} %bitcast.4, bf16[16,128]{1,0:T(8,128)(2,1)} %filt.1, bf16[2,128]{1,0:T(2,128)(2,1)} %bitcast.5, bf16[512,256]{1,0:T(8,128)(2,1)} %cot.1), custom_call_target="tpu_custom_call" | custom-call | tf_op jit(solution)/shard_map/pallas_call | solution.py:500
  50.6 1.4 %shard_map.77 = (f32[3,7,256]{2,1,0:T(8,128)}, f32[16,128]{1,0:T(8,128)}, f32[1,256]{1,0:T(1,128)}) custom-call(f32[64,128]{1,0:T(8,128)} %shard_map.76.packed), custom_call_target="tpu_custom_call" | custom-call | tf_op jit(solution)/shard_map/pallas_call | solution.py:509

commit v4 on v3

--- a/solution.py
+++ b/solution.py
@@ -41,8 +41,8 @@
 
 def kernel(geo, proj, taps, filt, skip, cot, out,
            pb, cb, tr, lf, sk, lff, wv, pf, kv, qv, xt, qt, gt, innt, ut, wt, inn, tof, tob, xg,
-           pgt, skt, at, bt, st, acc, bases, slr, sly, slz,
-           ld_sem, h_s, h_r, s_s, s_r, a_s, a_r, b_s, b_r, c_s, c_r):
+           pgt, skt, at, bt, st, st2, acc, tots, bases, slr, sly, slz,
+           ld_sem, h_s, h_r, s_s, s_r, t_s, t_r, a_s, a_r, b_s, b_r, c_s, c_r):
     n_seq, n_dp, n_y, n_z, rows, n_taps, channels = geo
     blocks = rows // LANES
     groups = channels // MEMBERS
@@ -167,7 +167,6 @@
         query_block(block)
 
     lff[...] = lf[...].astype(F32)
-    row8 = iota((8, LANES), 0)
     row_all = iota((8 * groups, LANES), 0)
     keep = iota((LANES, LANES), 1) >= iota((LANES, LANES), 0)
     base = jnp.concatenate(
@@ -195,6 +194,48 @@
         line = jnp.broadcast_to(sk[ct : ct + 1, :].astype(F32), (LANES, LANES))
         skt[cols, :] = line.T
 
+    zero8 = jnp.zeros((8, LANES), F32)
+    split = blocks // 2
+
+    def forward(begin, end):
+        def run(g, sums):
+            sums = list(sums)
+            r = pl.ds(aligned(g, MEMBERS), MEMBERS)
+            source = [xt[r, b * LANES : (b + 1) * LANES] for b in range(begin, end + 1)]
+            left = jnp.concatenate(
+                [jnp.concatenate(source[b : b + 2], axis=1) for b in range(end - begin)], axis=0)
+            filtered = dot(left, tof[g])
+            gain = skt[r, :]
+            for b in range(end - begin):
+                cols = slice((begin + b) * LANES, (begin + b + 1) * LANES)
+                inner = filtered[b * MEMBERS : (b + 1) * MEMBERS] + gain * source[b + 1].astype(F32)
+                queries = qt[r, cols]
+                output = queries * inner
+                cotangent = gt[r, cols]
+                sums[b] = sums[b] + fold(output * output)
+                sums[end - begin + b] = sums[end - begin + b] + fold(cotangent * output)
+                innt[r, cols] = inner
+                ut[r, cols] = cotangent * queries
+                wt[r, cols] = output * queries
+            return tuple(sums)
+
+        sums = lax.fori_loop(0, groups, run, (zero8,) * (2 * (end - begin)), unroll=8)
+        return jnp.concatenate([jnp.sum(part, axis=0, keepdims=True) for part in sums], axis=0)
+
+    def stat_copy(slots, sends, receives, i, index=None):
+        place = md if index is None else index
+        return pltpu.make_async_remote_copy(
+            src_ref=slots.at[place], dst_ref=slots.at[place], send_sem=sends.at[i],
+            recv_sem=receives.at[place], device_id=dp_peer(i), device_id_type=MESH)
+
+    def send_stats(slots, sends, receives):
+        @pl.loop(1, n_dp)
+        def _(i):
+            stat_copy(slots, sends, receives, i).start()
+
+    st2[md] = forward(split, blocks)
+    send_stats(st2, t_s, t_r)
+
     @pl.when(me > 0)
     def _():
         halo[0].wait_recv()
@@ -216,40 +257,8 @@
     def _():
         halo[1].wait_recv()
 
-    zero8 = jnp.zeros((8, LANES), F32)
-
-    def forward(g, sums):
-        sums = list(sums)
-        r = pl.ds(aligned(g, MEMBERS), MEMBERS)
-        source = [xt[r, b * LANES : (b + 1) * LANES] for b in range(blocks + 1)]
-        left = jnp.concatenate(
-            [jnp.concatenate([source[b], source[b + 1]], axis=1) for b in range(blocks)], axis=0)
-        filtered = dot(left, tof[g])
-        gain = skt[r, :]
-        for b in range(blocks):
-            cols = slice(b * LANES, (b + 1) * LANES)
-            inner = filtered[b * MEMBERS : (b + 1) * MEMBERS] + gain * source[b + 1].astype(F32)
-            queries = qt[r, cols]
-            output = queries * inner
-            cotangent = gt[r, cols]
-            sums[b] = sums[b] + fold(output * output)
-            sums[blocks + b] = sums[blocks + b] + fold(cotangent * output)
-            innt[r, cols] = inner
-            ut[r, cols] = cotangent * queries
-            wt[r, cols] = output * queries
-        return tuple(sums)
-
-    sums = lax.fori_loop(0, groups, forward, (zero8,) * (2 * blocks), unroll=8)
-    st[md] = jnp.concatenate([jnp.sum(part, axis=0, keepdims=True) for part in sums], axis=0)
-
-    def stat_copy(i):
-        return pltpu.make_async_remote_copy(
-            src_ref=st.at[md], dst_ref=st.at[md], send_sem=s_s.at[i],
-            recv_sem=s_r.at[md], device_id=dp_peer(i), device_id_type=MESH)
-
-    @pl.loop(1, n_dp)
-    def _(i):
-        stat_copy(i).start()
+    st[md] = forward(0, split)
+    send_stats(st, s_s, s_r)
 
     @pl.loop(0, blocks)
     def _(block):
@@ -257,12 +266,14 @@
         for ct in range(cts):
             inn[ct, here, :] = innt[ct * LANES : (ct + 1) * LANES, here].T
 
-    @pl.loop(0, groups)
-    def _(g):
+    def stack_blocks(g, carry):
         r = pl.ds(aligned(g, MEMBERS), MEMBERS)
         stack = [xt[r, b * LANES : (b + 1) * LANES].astype(F32) for b in range(blocks + 1)]
         stack.append(jnp.zeros((LANES - (blocks + 1) * MEMBERS, LANES), F32))
         xg[g] = jnp.concatenate(stack, axis=0).T.astype(BF16)
+        return carry
+
+    lax.fori_loop(0, groups, stack_blocks, 0, unroll=4)
 
     @pl.when(me > 0)
     def _():
@@ -273,99 +284,123 @@
         for p in (1, 2):
             kv[(p - 1) * cts + ct, 0:LANES, :] = featured(p, ct, 0)
 
-    @pl.loop(1, n_dp)
-    def _(i):
-        src = lax.rem(md + i, n_dp)
-        pltpu.make_async_remote_copy(
-            src_ref=st.at[src], dst_ref=st.at[src], send_sem=s_s.at[i],
-            recv_sem=s_r.at[src], device_id=dp_peer(i), device_id_type=MESH).wait_recv()
-
-    whole = st[0]
-    for i in range(1, n_dp):
-        whole = whole + st[i]
-    mean = whole * (1.0 / (channels * n_dp))
     token_scale = 1.0 / math.sqrt(rows * n_seq)
-    rms = jnp.sqrt(mean[0:blocks] + 1e-05)
-    scale_a = token_scale / rms
-    scale_b = token_scale * mean[blocks : 2 * blocks] / (rms * rms * rms)
-    lines_a = [scale_a[b : b + 1] for b in range(blocks)]
-    lines_b = [scale_b[b : b + 1] for b in range(blocks)]
-    for b in range(blocks):
-        at[b] = jnp.broadcast_to(lines_a[b], (LANES, LANES)).T
-        bt[b] = jnp.broadcast_to(lines_b[b], (LANES, LANES)).T
-
-    pad = jnp.zeros((MEMBERS, LANES), BF16)
-    fill = jnp.zeros((LANES - (blocks + 1) * MEMBERS, LANES), BF16)
-
-    def backward(g, carry):
-        r = pl.ds(aligned(g, MEMBERS), MEMBERS)
-        parts = []
-        for b in range(blocks):
-            cols = slice(b * LANES, (b + 1) * LANES)
-            parts.append((ut[r, cols] * lines_a[b] - wt[r, cols] * lines_b[b]).astype(BF16))
-        chain = [pad] + parts + [pad]
-        left = jnp.concatenate(
-            [jnp.concatenate([chain[b], chain[b + 1]], axis=1) for b in range(blocks + 1)], axis=0)
-        grad = dot_nt(left, tob[g])
-        for b in range(blocks + 1):
-            pgt[r, b * LANES : (b + 1) * LANES] = grad[b * MEMBERS : (b + 1) * MEMBERS]
-        right = jnp.concatenate(
-            [jnp.concatenate(parts + [pad, fill], axis=0), jnp.concatenate([pad] + parts + [fill], axis=0)],
-            axis=1)
-        lagged = dot(xg[g], right)
-        square = jnp.where(keep, lagged[:, LANES:], lagged[:, :LANES])
-        total = square[0:8]
-        for t in range(1, LANES // 8):
-            total = total + pltpu.roll(square[8 * t : 8 * t + 8], LANES - 8 * t, 1)
-        bases[pl.ds(aligned(g, 8), 8), :] = total
-        return carry
-
-    lax.fori_loop(0, groups, backward, 0, unroll=8)
+
+    def scales(slots, sends, receives, begin, end):
+        @pl.loop(1, n_dp)
+        def _(i):
+            stat_copy(slots, sends, receives, i, lax.rem(md + i, n_dp)).wait_recv()
+
+        whole = slots[0]
+        for i in range(1, n_dp):
+            whole = whole + slots[i]
+        count = end - begin
+        mean = whole * (1.0 / (channels * n_dp))
+        rms = jnp.sqrt(mean[0:count] + 1e-05)
+        scale_a = token_scale / rms
+        scale_b = token_scale * mean[count : 2 * count] / (rms * rms * rms)
+        lines_a = [scale_a[b : b + 1] for b in range(count)]
+        lines_b = [scale_b[b : b + 1] for b in range(count)]
+        for b in range(count):
+            at[begin + b] = jnp.broadcast_to(lines_a[b], (LANES, LANES)).T
+            bt[begin + b] = jnp.broadcast_to(lines_b[b], (LANES, LANES)).T
+        return lines_a, lines_b
+
+    def backward(lines_a, lines_b, begin, end, first):
+        pad = jnp.zeros((MEMBERS, LANES), BF16)
+
+        def padded(before, parts):
+            after = LANES - before - len(parts) * MEMBERS
+            return jnp.concatenate(
+                [jnp.zeros((before, LANES), BF16)] * (before > 0) + parts + [jnp.zeros((after, LANES), BF16)],
+                axis=0)
+
+        def run(g, carry):
+            r = pl.ds(aligned(g, MEMBERS), MEMBERS)
+            parts = []
+            for b in range(begin, end):
+                cols = slice(b * LANES, (b + 1) * LANES)
+                parts.append(
+                    (ut[r, cols] * lines_a[b - begin] - wt[r, cols] * lines_b[b - begin]).astype(BF16))
+            chain = [pad] + parts + [pad]
+            left = jnp.concatenate(
+                [jnp.concatenate(chain[b : b + 2], axis=1) for b in range(len(chain) - 1)], axis=0)
+            grad = dot_nt(left, tob[g])
+            for b in range(begin, end + 1):
+                cols = slice(b * LANES, (b + 1) * LANES)
+                piece = grad[(b - begin) * MEMBERS : (b - begin + 1) * MEMBERS]
+                if b == end and not first:
+                    piece = piece + pgt[r, cols]
+                pgt[r, cols] = piece
+            right = jnp.concatenate(
+                [padded(begin * MEMBERS, parts), padded((begin + 1) * MEMBERS, parts)], axis=1)
+            lagged = dot(xg[g], right)
+            square = jnp.where(keep, lagged[:, LANES:], lagged[:, :LANES])
+            total = square[0:8]
+            for t in range(1, LANES // 8):
+                total = total + pltpu.roll(square[8 * t : 8 * t + 8], LANES - 8 * t, 1)
+            place = pl.ds(aligned(g, 8), 8)
+            bases[place, :] = total if first else bases[place, :] + total
+            return carry
+
+        lax.fori_loop(0, groups, run, 0, unroll=8)
+
+    def tail(ct, block, totals, inside):
+        cols = slice(ct * LANES, (ct + 1) * LANES)
+        gain = sk[ct : ct + 1, :].astype(F32)
+        totals = list(totals)
+        here = pl.ds(aligned(block, LANES), LANES)
+        backed = pgt[cols, here].T
+        windows = [
+            pf.at[p * cts + ct, pl.ds(aligned(block, LANES), LANES + 16), :] for p in range(3)]
+        step = 32
+
+        def taps_of(part, begin, grad):
+            for j in range(n_taps):
+                term = grad * windows[part][16 - j + begin : 16 - j + begin + step, :]
+                totals[part * 8 + j] = totals[part * 8 + j] + fold(term)
+
+        for begin in range(0, LANES, step):
+            local = pl.ds(pl.multiple_of(block * LANES + begin, 8), step)
+            keys = kv[ct, local, :]
+            values = kv[cts + ct, local, :]
+            grad = backed[begin : begin + step]
+            if inside:
+                own = pl.ds(pl.multiple_of((block - 1) * LANES + begin, 16), step)
+                queries = qv[ct, own, :]
+                inner = inn[ct, own, :]
+                first = at[block - 1, begin : begin + step, :]
+                second = bt[block - 1, begin : begin + step, :]
+                out_grad = cb[own, cols].astype(F32) * first - queries * inner * second
+                conv = out_grad * queries
+                grad = grad + gain * conv
+                product = (keys * values).astype(BF16).astype(F32)
+                totals[7] = totals[7] + fold(conv * product)
+                taps_of(0, begin, out_grad * inner)
+            taps_of(1, begin, grad * values)
+            taps_of(2, begin, grad * keys)
+        return tuple(totals)
+
+    lines = scales(st2, t_s, t_r, split, blocks)
+    backward(*lines, split, blocks, True)
+    for ct in range(cts):
+        totals = lax.fori_loop(
+            split + 1, blocks + 1, lambda block, sums: tail(ct, block, sums, True), (zero8,) * 24)
+        for n in range(24):
+            tots[ct, n] = totals[n]
+
+    lines = scales(st, s_s, s_r, 0, split)
+    backward(*lines, 0, split, False)
+    row_all = iota((8 * groups, LANES), 0)
     lag = bases[...]
     for k in (1, 2, 4):
         lag = jnp.where((row_all & k) != 0, pltpu.roll(lag, LANES - k, 1), lag)
     acc[48 : 48 + groups, :] = jnp.concatenate(
         [jnp.sum(lag[8 * g : 8 * g + 8], axis=0, keepdims=True) for g in range(groups)], axis=0)
-
     for ct in range(cts):
-        cols = slice(ct * LANES, (ct + 1) * LANES)
-        gain = sk[ct : ct + 1, :].astype(F32)
-
-        def taps_of(part, window, begin, count, grad, totals):
-            for j in range(n_taps):
-                term = grad * window[16 - j + begin : 16 - j + begin + count, :]
-                totals[part * 8 + j] = totals[part * 8 + j] + fold(term)
-
-        def tail(block, totals, inside):
-            totals = list(totals)
-            here = pl.ds(aligned(block, LANES), LANES)
-            backed = pgt[cols, here].T
-            windows = [
-                pf.at[p * cts + ct, pl.ds(aligned(block, LANES), LANES + 16), :] for p in range(3)]
-            step = 32
-            for begin in range(0, LANES, step):
-                local = pl.ds(pl.multiple_of(block * LANES + begin, 8), step)
-                keys = kv[ct, local, :]
-                values = kv[cts + ct, local, :]
-                grad = backed[begin : begin + step]
-                if inside:
-                    own = pl.ds(pl.multiple_of((block - 1) * LANES + begin, 16), step)
-                    queries = qv[ct, own, :]
-                    inner = inn[ct, own, :]
-                    first = at[block - 1, begin : begin + step, :]
-                    second = bt[block - 1, begin : begin + step, :]
-                    out_grad = cb[own, cols].astype(F32) * first - queries * inner * second
-                    conv = out_grad * queries
-                    grad = grad + gain * conv
-                    product = (keys * values).astype(BF16).astype(F32)
-                    totals[7] = totals[7] + fold(conv * product)
-                    taps_of(0, windows[0], begin, step, out_grad * inner, totals)
-                taps_of(1, windows[1], begin, step, grad * values, totals)
-                taps_of(2, windows[2], begin, step, grad * keys, totals)
-            return tuple(totals)
-
-        totals = tail(0, (zero8,) * 24, False)
-        totals = lax.fori_loop(1, blocks + 1, functools.partial(tail, inside=True), totals)
+        totals = tail(ct, 0, [tots[ct, n] for n in range(24)], False)
+        totals = lax.fori_loop(
+            1, split + 1, lambda block, sums: tail(ct, block, sums, True), totals)
         for p in range(3):
             acc[(p * cts + ct) * 8 : (p * cts + ct) * 8 + 8, :] = jnp.concatenate(
                 [jnp.sum(totals[p * 8 + j], axis=0, keepdims=True) for j in range(8)], axis=0)
@@ -416,7 +451,8 @@
 
     @pl.loop(1, n_dp)
     def _(i):
-        stat_copy(i).wait_send()
+        stat_copy(st, s_s, s_r, i).wait_send()
+        stat_copy(st2, t_s, t_r, i).wait_send()
 
     swap.wait_send()
 
@@ -484,13 +520,16 @@
         vmem((channels, LANES), F32),
         vmem((blocks, LANES, LANES), F32),
         vmem((blocks, LANES, LANES), F32),
-        vmem((n_dp, 8, LANES), F32),
+        vmem((n_dp, blocks // 2 * 2, LANES), F32),
+        vmem((n_dp, blocks // 2 * 2, LANES), F32),
         vmem((64, LANES), F32),
+        vmem((cts, 24, 8, LANES), F32),
         vmem((8 * groups, LANES), F32),
         vmem((32, LANES), F32),
         vmem((n_y, 32, LANES), BF16),
         vmem((n_z, 32, LANES), BF16),
         dma((5,)), dma((3,)), dma((3,)),
+        dma((n_dp,)), dma((n_dp,)),
         dma((n_dp,)), dma((n_dp,)),
         dma((1,)), dma((1,)),
         dma((n_y,)), dma((n_y,)),

time: 52.2 us -> 51.4 us (0.985)
  Pallas kernels: 51.4 us -> 50.6 us
    pallas_call x1, Pallas kernels: 50 us -> 49.2 us  [body(): pl.pallas_call(functools.partial(kernel, geo), out_shape=jax.ShapeDtypeSt...]
where the time goes in v4:
time: 51.4 us; the launch traced here: 51.2 us
  Pallas kernels  50.6 us (98%)
  between operations  0.64 us (1%)
    pallas_call x1, Pallas kernels, body(): pl.pallas_call(functools.partial(kernel, geo), out_shape=jax.ShapeDtypeSt...  49.2 us
    pallas_call x1, Pallas kernels, body(): pl.pallas_call(unpack, out_shape=(jax.ShapeDtypeStruct((parts, n_taps, ch...  1.38 us

profile of v4, /device:TPU:1, one launch (start us, length us, event | category | flops | bytes accessed | tf_op | source)
XLA Modules:
  0.0 51.2 jit_solution(1704772702553907507)
XLA Ops:
  0.6 49.2 %shard_map.76.packed = f32[64,128]{1,0:T(8,128)} custom-call(bf16[3,512,256]{2,1,0:T(8,128)(2,1)} %proj.1, bf16[3,7,256]{2,1,0:T(8,128)(2,1)} %bitcast.4, bf16[16,128]{1,0:T(8,128)(2,1)} %filt.1, bf16[2,128]{1,0:T(2,128)(2,1)} %bitcast.5, bf16[512,256]{1,0:T(8,128)(2,1)} %cot.1), custom_call_target="tpu_custom_call" | custom-call | tf_op jit(solution)/shard_map/pallas_call | solution.py:539
  49.8 1.4 %shard_map.77 = (f32[3,7,256]{2,1,0:T(8,128)}, f32[16,128]{1,0:T(8,128)}, f32[1,256]{1,0:T(1,128)}) custom-call(f32[64,128]{1,0:T(8,128)} %shard_map.76.packed), custom_call_target="tpu_custom_call" | custom-call | tf_op jit(solution)/shard_map/pallas_call | solution.py:548

commit v5 on v4

--- a/solution.py
+++ b/solution.py
@@ -58,8 +58,15 @@
         pltpu.make_async_copy(filt, lf, ld_sem.at[0]),
         pltpu.make_async_copy(taps, tr, ld_sem.at[1]),
         pltpu.make_async_copy(skip, sk, ld_sem.at[2]),
-        pltpu.make_async_copy(proj, pb.at[:, pl.ds(HALO, rows), :], ld_sem.at[3]),
+        pltpu.make_async_copy(
+            proj.at[pl.ds(1, 2), pl.ds(rows - HALO, HALO), :],
+            pb.at[pl.ds(1, 2), pl.ds(rows, HALO), :], ld_sem.at[3]),
         pltpu.make_async_copy(cot, cb, ld_sem.at[4]),
+        pltpu.make_async_copy(
+            proj.at[pl.ds(1, 2), pl.ds(0, rows - HALO), :],
+            pb.at[pl.ds(1, 2), pl.ds(HALO, rows - HALO), :], ld_sem.at[5]),
+        pltpu.make_async_copy(
+            proj.at[pl.ds(0, 1), :, :], pb.at[pl.ds(0, 1), pl.ds(HALO, rows), :], ld_sem.at[6]),
     ]
     barrier = pltpu.get_barrier_semaphore()
 
@@ -103,8 +110,8 @@
             total = term if total is None else total + term
         return total.astype(BF16).astype(F32)
 
-    def widen(begin, count):
-        for p in range(3):
+    def widen(begin, count, parts=(0, 1, 2)):
+        for p in parts:
             for ct in range(cts):
                 pf[p * cts + ct, pl.ds(begin, count), :] = pb[
                     p, pl.ds(begin, count), ct * LANES : (ct + 1) * LANES].astype(F32)
@@ -131,10 +138,7 @@
 
     loads[3].wait()
 
-    @pl.loop(0, blocks)
-    def _(block):
-        widen(pl.multiple_of(HALO + block * LANES, 16), LANES)
-
+    widen(rows, HALO, (1, 2))
     product_block(blocks)
 
     pl.semaphore_wait(barrier, n_dp + n_y + n_z - 1)
@@ -156,7 +160,10 @@
         halo[0].start()
         halo[1].start()
 
-    loads[4].wait()
+    for copy in loads[4:]:
+        copy.wait()
+    widen(HALO, rows - HALO, (1, 2))
+    widen(HALO, rows, (0,))
 
     @pl.loop(2, blocks)
     def _(block):
@@ -528,7 +535,7 @@
         vmem((32, LANES), F32),
         vmem((n_y, 32, LANES), BF16),
         vmem((n_z, 32, LANES), BF16),
-        dma((5,)), dma((3,)), dma((3,)),
+        dma((7,)), dma((3,)), dma((3,)),
         dma((n_dp,)), dma((n_dp,)),
         dma((n_dp,)), dma((n_dp,)),
         dma((1,)), dma((1,)),

time: 51.4 us -> 51.5 us (level)
  no operation moved by 1% of the time
where the time goes in v5:
time: 51.5 us; the launch traced here: 51.3 us
  Pallas kernels  50.6 us (98%)
  between operations  0.64 us (1%)
    pallas_call x1, Pallas kernels, body(): pl.pallas_call(functools.partial(kernel, geo), out_shape=jax.ShapeDtypeSt...  49.2 us
    pallas_call x1, Pallas kernels, body(): pl.pallas_call(unpack, out_shape=(jax.ShapeDtypeStruct((parts, n_taps, ch...  1.38 us

profile of v5, /device:TPU:1, one launch (start us, length us, event | category | flops | bytes accessed | tf_op | source)
XLA Modules:
  0.0 51.3 jit_solution(9154367315360871415)
XLA Ops:
  0.6 49.2 %shard_map.76.packed = f32[64,128]{1,0:T(8,128)} custom-call(bf16[3,512,256]{2,1,0:T(8,128)(2,1)} %proj.1, bf16[3,7,256]{2,1,0:T(8,128)(2,1)} %bitcast.4, bf16[16,128]{1,0:T(8,128)(2,1)} %filt.1, bf16[2,128]{1,0:T(2,128)(2,1)} %bitcast.5, bf16[512,256]{1,0:T(8,128)(2,1)} %cot.1), custom_call_target="tpu_custom_call" | custom-call | tf_op jit(solution)/shard_map/pallas_call | solution.py:546
  49.9 1.4 %shard_map.77 = (f32[3,7,256]{2,1,0:T(8,128)}, f32[16,128]{1,0:T(8,128)}, f32[1,256]{1,0:T(1,128)}) custom-call(f32[64,128]{1,0:T(8,128)} %shard_map.76.packed), custom_call_target="tpu_custom_call" | custom-call | tf_op jit(solution)/shard_map/pallas_call | solution.py:555

commit v6 on v4

--- a/solution.py
+++ b/solution.py
@@ -30,6 +30,13 @@
 
 def aligned(index, step):
     return pl.multiple_of(index * step, step)
+
+
+def far_first(count, ring, step):
+    def distance(i):
+        return min(i % ring, ring - i % ring) // step
+
+    return sorted(range(1, count), key=distance, reverse=True)
 
 
 def fold(array):
@@ -229,8 +236,7 @@
             recv_sem=receives.at[place], device_id=dp_peer(i), device_id_type=MESH)
 
     def send_stats(slots, sends, receives):
-        @pl.loop(1, n_dp)
-        def _(i):
+        for i in far_first(n_dp, n_dp // 2, 1):
             stat_copy(slots, sends, receives, i).start()
 
     st2[md] = forward(split, blocks)
@@ -422,8 +428,7 @@
     swap.wait_recv()
     sly[my] = (acc[pl.ds(aligned(core, half), half), :] + slr[...]).astype(BF16)
 
-    @pl.loop(1, n_y)
-    def _(i):
+    for i in far_first(n_y, n_y, 1):
         exchange(sly, b_s, b_r, my, i, y_peer).start()
 
     @pl.loop(1, n_y)
@@ -435,8 +440,7 @@
         part = part + sly[i].astype(F32)
     slz[mz] = part.astype(BF16)
 
-    @pl.loop(1, n_z)
-    def _(i):
+    for i in far_first(n_z, n_z, 2):
         exchange(slz, c_s, c_r, mz, i, z_peer).start()
 
     @pl.loop(1, n_z)

time: 51.4 us -> 51 us (level)
  no operation moved by 1% of the time
where the time goes in v6:
time: 51 us; the launch traced here: 50.8 us
  Pallas kernels  50.1 us (98%)
  between operations  0.64 us (1%)
    pallas_call x1, Pallas kernels, body(): pl.pallas_call(functools.partial(kernel, geo), out_shape=jax.ShapeDtypeSt...  48.8 us
    pallas_call x1, Pallas kernels, body(): pl.pallas_call(unpack, out_shape=(jax.ShapeDtypeStruct((parts, n_taps, ch...  1.38 us

profile of v6, /device:TPU:1, one launch (start us, length us, event | category | flops | bytes accessed | tf_op | source)
XLA Modules:
  0.0 50.8 jit_solution(18104948092852877733)
XLA Ops:
  0.6 48.8 %shard_map.76.packed = f32[64,128]{1,0:T(8,128)} custom-call(bf16[3,512,256]{2,1,0:T(8,128)(2,1)} %proj.1, bf16[3,7,256]{2,1,0:T(8,128)(2,1)} %bitcast.4, bf16[16,128]{1,0:T(8,128)(2,1)} %filt.1, bf16[2,128]{1,0:T(2,128)(2,1)} %bitcast.5, bf16[512,256]{1,0:T(8,128)(2,1)} %cot.1), custom_call_target="tpu_custom_call" | custom-call | tf_op jit(solution)/shard_map/pallas_call | solution.py:543
  49.4 1.4 %shard_map.77 = (f32[3,7,256]{2,1,0:T(8,128)}, f32[16,128]{1,0:T(8,128)}, f32[1,256]{1,0:T(1,128)}) custom-call(f32[64,128]{1,0:T(8,128)} %shard_map.76.packed), custom_call_target="tpu_custom_call" | custom-call | tf_op jit(solution)/shard_map/pallas_call | solution.py:552
